TPU v7x, 512 devices: a whole 4x8x8 slice. The times are simulated.
512 devices in a mesh: ctx: 64 (over y_hi, z, core), hs: 8 (over y_lo, x).
Axes of the slice: x: 4, y: 8 (y_hi: 4, y_lo: 2; y = y_hi * 2 + y_lo), z: 8, core: 2. Of those that a mesh axis runs over, the one named last changes fastest.
Arguments:
- queries: bfloat16 [8192, 36864], P('ctx', 'hs'), may hold values from -210 to 210
- grad_out: bfloat16 [8192, 32768], P('ctx', 'hs'), may hold values from -6 to 6
- prompt_kv: bfloat16 [576, 1024], P(None, 'hs'), may hold values from -6 to 6
- comp_kv: bfloat16 [576, 8192], P(None, 'ctx'), may hold values from -6 to 6
- lengths: int32 [64], replicated, may hold values from 32 to 128, as said below
Outputs:
- grad_queries: bfloat16 [8192, 36864], P('ctx', 'hs')
- grad_prompt: float32 [576, 1024], P(None, 'hs')
- grad_comp: float32 [576, 8192], P(None, 'ctx')
Inputs may be any that keep to these rules, and one draw needn't show every extreme that they name: lengths[s] slots of completion s are live, the rest of its 128 slots are padding; some completion fills all 128 slots.
All inputs are finite; a program needn't handle non-finite values.
Results may differ from a plain program's by a relative error of at most 0.012.
Values may be sent and summed in bfloat16 or wider, within the bound.
No kernel may reach another device: no remote copies, remote signals or barrier semaphores. Data moves between devices by JAX's collectives and lax.ppermute only.
A program may use at most 64 MiB of HBM per device.

v0:
```python
import jax
import jax.numpy as jnp
from jax import lax
from jax.sharding import PartitionSpec as P

D_LAT = 512
DQK = 576


score_scale = 192.0 ** (-0.5)


def on_device(queries, grad_out, prompt_kv, comp_kv, lengths):
    slot_count = queries.shape[0]
    head_count = queries.shape[1] // DQK
    head_queries = queries.reshape(slot_count, head_count, DQK)
    cotangent = grad_out.reshape(slot_count, head_count, D_LAT)
    sample = lax.axis_index("ctx")
    live_len = jnp.sum(jnp.where(jnp.arange(lengths.shape[0]) == sample, lengths, 0))
    prompt_all = lax.all_gather(prompt_kv, "hs", axis=1, tiled=True)
    prompt_len = prompt_all.shape[1]
    keys_all = jnp.concatenate([prompt_all, comp_kv], axis=1)
    values_all = keys_all[:D_LAT]
    position = jnp.arange(slot_count)
    key_index = jnp.arange(prompt_len + slot_count)
    allowed = key_index[None, :] < prompt_len + position[:, None] + 1
    scores = (
        jnp.einsum("thd,dk->thk", head_queries, keys_all, preferred_element_type=jnp.float32)
        * score_scale
    )
    scores = jnp.where(allowed[:, None, :], scores, -jnp.inf)
    largest = jnp.max(scores, axis=-1, keepdims=True)
    weights = jnp.exp(scores - largest)
    probability = weights / jnp.sum(weights, axis=-1, keepdims=True)
    live_rows = (position < live_len).astype(jnp.float32)[:, None, None]
    live_prob = probability * live_rows
    kept_probs = live_prob.astype(jnp.bfloat16)
    grad_prob = jnp.einsum("the,ek->thk", cotangent, values_all, preferred_element_type=jnp.float32)
    row_delta = jnp.sum(live_prob * grad_prob, axis=-1, keepdims=True)
    grad_score = (live_prob * (grad_prob - row_delta)).astype(jnp.bfloat16)
    grad_q = (
        jnp.einsum("thk,dk->thd", grad_score, keys_all, preferred_element_type=jnp.float32)
        * score_scale
    )
    grad_queries = grad_q.astype(jnp.bfloat16).reshape(slot_count, head_count * DQK)
    key_part = (
        jnp.einsum("thk,thd->dk", grad_score, head_queries, preferred_element_type=jnp.float32)
        * score_scale
    )
    value_part = jnp.einsum(
        "thk,the->ek", kept_probs, cotangent, preferred_element_type=jnp.float32
    )
    key_grads = key_part.at[:D_LAT].add(value_part)
    prompt_term = key_grads[:, :prompt_len]
    comp_term = key_grads[:, prompt_len:]
    summed = lax.psum(prompt_term, "ctx")
    grad_prompt = lax.psum_scatter(summed, "hs", scatter_dimension=1, tiled=True)
    grad_comp = lax.psum(comp_term, "hs")
    return (grad_queries, grad_prompt, grad_comp)


def solution(mesh):
    in_specs = (P("ctx", "hs"), P("ctx", "hs"), P(None, "hs"), P(None, "ctx"), P())
    out_specs = (P("ctx", "hs"), P(None, "hs"), P(None, "ctx"))
    return jax.shard_map(
        on_device, mesh=mesh, in_specs=in_specs, out_specs=out_specs, check_vma=False
    )
```

profile of v0, /device:TPU:1, one launch (start us, length us, event | category | flops | bytes accessed | tf_op | source)
XLA Modules:
  0.0 745.0 jit_solution(13563323010602704790)
XLA Ops:
  7.2 0.0 copy-start.2
  7.2 0.0 copy-start.11
  7.2 0.0 all-gather.2.cloned.1.call-start
  7.2 0.7 all-gather.2.cloned.1.call-update
  7.9 0.0 reduce-scatter.2.cloned.1.call-start
  8.0 1.6 copy.30
  9.6 0.0 copy-done.2
  9.6 0.0 copy-start.6
  9.6 0.7 copy.17
  10.3 0.0 copy-start.3
  10.4 0.0 copy-done.11
  10.4 0.8 fusion.16
  11.1 0.6 compare_convert_fusion
  11.8 0.0 copy-start.9
  11.8 0.1 iota_compare_fusion
  11.9 43.0 %all-gather.2.cloned.1.call-done = bf16[576,1024]{1,0:T(8,128)(2,1)} async-done(((bf16[576,128]{1,0:T(8,128)(2,1)}), bf16[576,1024]{1,0:T(8,128)(2,1)}) %all-gather.2.cloned.1.call-update) | async-done | bytes 1179664 | tf_op jit(solution)/shard_map/all_gather | solution.py:20
  54.9 1.4 constant_dynamic-update-slice_fusion.1
  56.3 0.9 constant_dynamic-update-slice_fusion
  57.2 0.0 copy-start.5
  57.3 2.1 convolution_multiply_fusion
  59.3 0.0 copy-done.3
  59.3 0.0 copy-start
  59.3 1.4 exponential_reduce_fusion
  60.7 0.7 copy-done
  61.4 0.0 copy-done.6
  61.4 0.0 copy-done.5
  61.5 2.0 fusion.2
  63.4 0.0 copy-done.9
  63.5 0.0 copy-start.4
  63.5 1.3 fusion.4
  64.7 1.4 copy-done.1
  66.2 0.0 copy-done.4
  66.2 1.7 fusion.7
  67.9 5.3 fusion.9
  73.2 1.7 slice.34
  74.9 0.0 reduce-scatter.2.cloned.1.call-update
  74.9 0.0 all-reduce.3.cloned.1.call-start
  75.0 0.7 slice.35
  75.7 0.0 all-reduce.3.cloned.1.call-update
  75.7 0.0 all-reduce.5.cloned.1.call-start
  75.8 48.1 %reduce-scatter.2.cloned.1.call-done = f32[576,128]{1,0:T(8,128)} async-done(((f32[576,1024]{1,0:T(8,128)}), f32[576,128]{1,0:T(8,128)}) %reduce-scatter.2.cloned.1.call-update) | async-done | bytes 294928 | tf_op jit(solution)/shard_map/reduce_scatter | solution.py:57
  123.9 0.0 all-reduce.5.cloned.1.call-update
  123.9 3.8 multiply_convert_fusion
  127.6 1.4 copy.24
  129.1 82.4 %all-reduce.3.cloned.1.call-done = f32[576,128]{1,0:T(8,128)} async-done(((f32[576,128]{1,0:T(8,128)}), f32[576,128]{1,0:T(8,128)}) %all-reduce.3.cloned.1.call-update) | async-done | bytes 294928 | tf_op jit(solution)/shard_map/psum | solution.py:58
  211.4 523.7 %all-reduce.5.cloned.1.call-done = f32[576,128]{1,0:T(8,128)} async-done(((f32[576,128]{1,0:T(8,128)}), f32[576,128]{1,0:T(8,128)}) %all-reduce.5.cloned.1.call-update) | async-done | bytes 294928 | tf_op jit(solution)/shard_map/psum | solution.py:56
  735.1 1.7 copy.35
  736.8 1.7 copy.36
  (8 shorter events, 0.0 us)
Async XLA Ops:
  7.2 2.4 copy-start.2
  7.2 3.2 copy-start.11
  7.2 47.8 %all-gather.2.cloned.1.call-start = ((), (), s32[]{:S(2)}) async-start(), calls=%async_computation.1 | async-start | bytes 1327104 | tf_op jit(solution)/shard_map/all_gather | solution.py:20
  7.9 115.9 %reduce-scatter.2.cloned.1.call-start = ((), (), s32[]{:S(2)}) async-start(), calls=%async_computation.3 | async-start | bytes 2654208 | tf_op jit(solution)/shard_map/reduce_scatter | solution.py:57
  9.6 51.8 %copy-start.6 = (bf16[128,4096]{0,1:T(8,128)(2,1)}, bf16[128,4096]{0,1:T(8,128)(2,1)S(1)}, u32[]{:S(2)}) copy-start(bf16[128,4096]{0,1:T(8,128)(2,1)S(1)} %copy.30) | copy-start | bytes 3145732
  10.3 49.0 %copy-start.3 = (bf16[128,4608]{0,1:T(8,128)(2,1)}, bf16[128,4608]{0,1:T(8,128)(2,1)S(1)}, u32[]{:S(2)}) copy-start(bf16[128,4608]{0,1:T(8,128)(2,1)S(1)} %copy.17) | copy-start | bytes 3538948
  11.8 51.6 %copy-start.9 = (f32[128]{0:T(128)}, f32[128]{0:T(128)S(1)}, u32[]{:S(2)}) copy-start(f32[128]{0:T(128)S(1)} %compare_convert_fusion) | copy-start | bytes 1540
  57.2 4.2 copy-start.5
  59.3 2.1 copy-start
  61.4 2.0 copy-start.7
  63.5 2.7 copy-start.4
  64.7 1.4 copy-start.1
  66.2 1.7 copy-start.8
  66.2 1.7 copy-start.10
  74.9 136.5 %all-reduce.3.cloned.1.call-start = ((), (), s32[]{:S(2)}) async-start(), calls=%async_computation.2 | async-start | bytes 589824 | tf_op jit(solution)/shard_map/psum | solution.py:58
  75.7 659.3 %all-reduce.5.cloned.1.call-start = ((), (), s32[]{:S(2)}) async-start(), calls=%async_computation.4 | async-start | bytes 589824 | tf_op jit(solution)/shard_map/psum | solution.py:56
Sparse Core Ops, SparseCore 0:
  10.0 44.8 all-gather.1
  75.1 48.7 reduce-scatter.1
  127.4 84.0 all-reduce.2
  214.4 520.5 all-reduce.4
where the time goes:
time: 745 us
  waiting for transfers between devices  698 us (94%)
  matrix products  14.8 us (2%)
  local copies, waits for them, and re-layouts  14.1 us (2%)
  between operations  14 us (2%)
    psum x1, waiting for transfers between devices, on_device(): summed = lax.psum(prompt_term, 'ctx')  524 us
    psum x1, waiting for transfers between devices, on_device(): grad_comp = lax.psum(comp_term, 'hs')  82.4 us
    reduce_scatter x1, waiting for transfers between devices, on_device(): lax.psum_scatter(summed, 'hs', scatter_dimension=1, tiled=True)  48.1 us
    all_gather x1, waiting for transfers between devices, on_device(): prompt_all = lax.all_gather(prompt_kv, 'hs', axis=1, tiled=True)  43 us
  transfers between devices with their start and end apart: 4, of which 4 were waited for; matrix products, arithmetic and copies ran while one was open for 1% of the time, Pallas kernels for 0%

commit v1 on v0

--- a/solution.py
+++ b/solution.py
@@ -1,13 +1,21 @@
 import jax
 import jax.numpy as jnp
 from jax import lax
+from jax.sharding import Mesh
 from jax.sharding import PartitionSpec as P
 
 D_LAT = 512
 DQK = 576
+HS = ("yl", "x")
+CTX = ("yh", "z", "c")
 
 
 score_scale = 192.0 ** (-0.5)
+
+
+def everyone(block, axes, count):
+    copies = jnp.broadcast_to(block[None], (count,) + block.shape)
+    return lax.all_to_all(copies, axes, 0, 0)
 
 
 def on_device(queries, grad_out, prompt_kv, comp_kv, lengths):
@@ -15,9 +23,10 @@
     head_count = queries.shape[1] // DQK
     head_queries = queries.reshape(slot_count, head_count, DQK)
     cotangent = grad_out.reshape(slot_count, head_count, D_LAT)
-    sample = lax.axis_index("ctx")
+    sample = lax.axis_index(CTX)
     live_len = jnp.sum(jnp.where(jnp.arange(lengths.shape[0]) == sample, lengths, 0))
-    prompt_all = lax.all_gather(prompt_kv, "hs", axis=1, tiled=True)
+    gathered = everyone(prompt_kv, HS, 8)
+    prompt_all = gathered.transpose(1, 0, 2).reshape(DQK, -1)
     prompt_len = prompt_all.shape[1]
     keys_all = jnp.concatenate([prompt_all, comp_kv], axis=1)
     values_all = keys_all[:D_LAT]
@@ -51,17 +60,25 @@
         "thk,the->ek", kept_probs, cotangent, preferred_element_type=jnp.float32
     )
     key_grads = key_part.at[:D_LAT].add(value_part)
-    prompt_term = key_grads[:, :prompt_len]
-    comp_term = key_grads[:, prompt_len:]
-    summed = lax.psum(prompt_term, "ctx")
-    grad_prompt = lax.psum_scatter(summed, "hs", scatter_dimension=1, tiled=True)
-    grad_comp = lax.psum(comp_term, "hs")
+    prompt_term = key_grads[:, :prompt_len].reshape(DQK, 8, -1).transpose(1, 0, 2)
+    comp_term = key_grads[:, prompt_len:].reshape(8, DQK // 8, -1)
+    terms = jnp.concatenate([prompt_term, comp_term], axis=1).astype(jnp.bfloat16)
+    terms = lax.all_to_all(terms, HS, 0, 0)
+    terms = jnp.sum(terms.astype(jnp.float32), axis=0).astype(jnp.bfloat16)
+    comp_rows = everyone(terms[DQK:], HS, 8)
+    grad_comp = comp_rows.reshape(DQK, -1).astype(jnp.float32)
+    pieces = lax.all_to_all(terms[:DQK].reshape(8, DQK // 8, -1), "z", 0, 0)
+    piece = jnp.sum(pieces.astype(jnp.float32), axis=0).astype(jnp.bfloat16)
+    pieces = everyone(piece, ("yh", "c"), 8)
+    piece = jnp.sum(pieces.astype(jnp.float32), axis=0).astype(jnp.bfloat16)
+    grad_prompt = everyone(piece, "z", 8).reshape(DQK, -1).astype(jnp.float32)
     return (grad_queries, grad_prompt, grad_comp)
 
 
 def solution(mesh):
-    in_specs = (P("ctx", "hs"), P("ctx", "hs"), P(None, "hs"), P(None, "ctx"), P())
-    out_specs = (P("ctx", "hs"), P(None, "hs"), P(None, "ctx"))
+    parts = Mesh(mesh.devices.reshape(4, 8, 2, 2, 4), CTX + HS)
+    in_specs = (P(CTX, HS), P(CTX, HS), P(None, HS), P(None, CTX), P())
+    out_specs = (P(CTX, HS), P(None, HS), P(None, CTX))
     return jax.shard_map(
-        on_device, mesh=mesh, in_specs=in_specs, out_specs=out_specs, check_vma=False
+        on_device, mesh=parts, in_specs=in_specs, out_specs=out_specs, check_vma=False
     )

time: 745 us -> 124 us (0.17)
  waiting for transfers between devices: 698 us -> 23.6 us
  blocking collectives: 0 us -> 45.2 us
  starting transfers between devices: 0.16 us -> 22.3 us
  between operations: 14 us -> 0.93 us
    psum x2 -> x0, waiting for transfers between devices: 606 us -> none  [the longest x1 524 us: on_device(): summed = lax.psum(prompt_term, 'ctx')]
    reduce_scatter x1 -> x0, waiting for transfers between devices: 48.1 us -> none  [on_device(): lax.psum_scatter(summed, 'hs', scatter_dimension=1, tiled=True)]
    all_to_all x0 -> x2, blocking collectives: none -> 45.2 us  [the longest x1 25.4 us: on_device(): terms = lax.all_to_all(terms, HS, 0, 0)]
    all_gather x1 -> x0, waiting for transfers between devices: 43 us -> none  [on_device(): prompt_all = lax.all_gather(prompt_kv, 'hs', axis=1, tiled=True)]
    all_to_all x0 -> x4, waiting for transfers between devices: none -> 23.6 us  [everyone(): return lax.all_to_all(copies, axes, 0, 0)]
    all_to_all x0 -> x4, starting transfers between devices: none -> 22.3 us  [everyone(): return lax.all_to_all(copies, axes, 0, 0)]
  transfers between devices with their start and end apart: 4 -> 4, of which waited for: 4 -> 4; matrix products, arithmetic and copies ran while one was open for 1% -> 7% of each run, Pallas kernels for 0% -> 0%
where the time goes in v1:
time: 124 us; the launch traced here: 123 us
  blocking collectives  45.2 us (36%)
  waiting for transfers between devices  23.6 us (19%)
  starting transfers between devices  22.3 us (18%)
  matrix products  14.4 us (12%)
  local copies, waits for them, and re-layouts  10.3 us (8%)
  other arithmetic  5.96 us (5%)
    all_to_all x1, blocking collectives, on_device(): terms = lax.all_to_all(terms, HS, 0, 0)  25.4 us
    all_to_all x4, waiting for transfers between devices, everyone(): return lax.all_to_all(copies, axes, 0, 0)  23.6 us
    all_to_all x4, starting transfers between devices, everyone(): return lax.all_to_all(copies, axes, 0, 0)  22.3 us
    all_to_all x1, blocking collectives, on_device(): pieces = lax.all_to_all(terms[:DQK].reshape(8, DQK // 8, -1), 'z', 0, 0)  19.8 us
    dot_general x1, matrix products, on_device(): jnp.einsum('thk,the->ek', kept_probs, cotangent, preferred_element_type=j...  5.35 us
    unnamed x27, local copies, waits for them, and re-layouts  4.48 us
    broadcast_in_dim x4, local copies, waits for them, and re-layouts, everyone(): copies = jnp.broadcast_to(block[None], (count,) + block.shape)  4.21 us
    dot_general x1, matrix products, on_device(): jnp.einsum('thk,dk->thd', grad_score, keys_all, preferred_element_type=jn...  3.35 us
  transfers between devices with their start and end apart: 4, of which 4 were waited for; matrix products, arithmetic and copies ran while one was open for 7% of the time, Pallas kernels for 0%

profile of v1, /device:TPU:1, one launch (start us, length us, event | category | flops | bytes accessed | tf_op | source)
XLA Modules:
  0.0 122.7 jit_solution(10895713923636960791)
XLA Ops:
  0.6 0.0 copy-start.7
  0.6 2.2 %broadcast_in_dim.25 = bf16[8,576,128]{2,1,0:T(8,128)(2,1)} broadcast(bf16[576,128]{1,0:T(8,128)(2,1)} %param.9), dimensions={1,2} | broadcast | bytes 1327104 | tf_op jit(solution)/shard_map/broadcast_in_dim | solution.py:17
  2.8 6.0 %all-to-all-start = ((bf16[8,576,128]{2,1,0:T(8,128)(2,1)}), bf16[8,576,128]{2,1,0:T(8,128)(2,1)S(1)}, u32[]{:S(2)}, u32[]{:S(2)}) async-start(bf16[8,576,128]{2,1,0:T(8,128)(2,1)} %broadcast_in_dim.25), calls=%async_computation | async-start | bytes 2359296 | tf_op jit(solution)/shard_map/all_to_all | solution.py:18
  8.8 0.0 copy-done.7
  8.8 1.3 %copy.52 = bf16[128,4096]{0,1:T(8,128)(2,1)} copy(bf16[128,4096]{1,0:T(8,128)(2,1)S(1)} %copy-done.7) | data formatting | bytes 2097152 | tf_op jit(solution)/shard_map/reshape | solution.py:25
  10.1 0.0 copy-done.2
  10.1 0.7 copy.38
  10.9 0.0 copy-start.3
  10.9 0.0 copy-start.10
  10.9 0.0 copy-done.11
  10.9 0.6 fusion.16
  11.5 0.6 compare_convert_fusion
  12.2 0.1 iota_compare_fusion
  12.3 0.0 copy-start.9
  12.3 7.3 %all-to-all-done = bf16[8,576,128]{2,1,0:T(8,128)(2,1)S(1)} async-done(((bf16[8,576,128]{2,1,0:T(8,128)(2,1)}), bf16[8,576,128]{2,1,0:T(8,128)(2,1)S(1)}, u32[]{:S(2)}, u32[]{:S(2)}) %all-to-all-start) | async-done | bytes 1179680 | tf_op jit(solution)/shard_map/all_to_all | solution.py:18
  19.7 0.1 bitcast_dynamic-update-slice_fusion
  19.8 0.0 copy-done.10
  19.8 0.0 copy-start.5
  19.9 2.0 %convolution_multiply_fusion = f32[1152,128,8]{1,0,2:T(8,128)S(1)} fusion(bf16[128,8,576]{0,2,1:T(8,128)(2,1)S(1)} %bitcast.76, bf16[576,1152]{1,0:T(8,128)(2,1)S(1)} %constant_dynamic-update-slice_fusion), kind=kOutput, calls=%fused_computation.2 | convolution fusion | flops 1360134144 | bytes 7225344 | tf_op jit(solution)/shard_map/thd,dk->thk/dot_general | solution.py:37
  21.9 0.0 copy-done.3
  21.9 0.0 copy-done.9
  21.9 1.4 %exponential_reduce_fusion = (f32[128,8]{0,1:T(8,128)S(1)}, f32[128,8,1152]{0,2,1:T(8,128)S(1)}) fusion(f32[1152,128,8]{1,0,2:T(8,128)S(1)} %convolution_multiply_fusion, pred[128,1152]{0,1:T(8,128)(4,1)S(1)} %iota_compare_fusion), kind=kOutput, calls=%fused_computation.11 | output fusion | flops 3540095 | bytes 9588736 | tf_op jit(solution)/shard_map/sub | solution.py:42
  23.3 0.7 copy-done
  24.1 2.0 %fusion.2 = (f32[128,8]{0,1:T(8,128)S(1)}, f32[1152,128,8]{1,0,2:T(8,128)S(1)}) fusion(f32[128]{0:T(128)S(1)} %compare_convert_fusion, f32[128,8]{0,1:T(8,128)S(1)} %get-tuple-element.27, f32[128,8,1152]{0,2,1:T(8,128)S(1)} %get-tuple-element.28, bf16[128,8,512]{0,2,1:T(8,128)(2,1)S(1)} %bitcast.80, bf16[576,1152]{1,0:T(8,128)(2,1)S(1)} %constant_dynamic-update-slice_fusion), kind=kOutput, calls=%fused_computation.5 | convolution fusion | flops 1212677120 | bytes 11674112 | tf_op jit(solution)/shard_map/the,ek->thk/dot_general | solution.py:47
  26.0 1.2 fusion.4
  27.3 0.0 copy-start.1
  27.3 1.4 %copy-done.1 = bf16[128,8,1152]{0,2,1:T(8,128)(2,1)} copy-done((bf16[128,8,1152]{0,2,1:T(8,128)(2,1)}, bf16[128,8,1152]{0,2,1:T(8,128)(2,1)S(1)}, u32[]{:S(2)}) %copy-start.1) | copy-done | bytes 2359320
  28.7 1.7 %fusion.7 = f32[576,1152]{1,0:T(8,128)S(1)} fusion(bf16[128,8,1152]{0,2,1:T(8,128)(2,1)S(1)} %fusion.4, bf16[128,8,576]{0,2,1:T(8,128)(2,1)S(1)} %bitcast.77), kind=kOutput, calls=%fused_computation.14 | convolution fusion | flops 1359618048 | bytes 6193152 | tf_op jit(solution)/shard_map/thk,thd->dk/dot_general | solution.py:56
  30.4 5.4 %fusion.9 = f32[576,1152]{1,0:T(8,128)S(1)} fusion(f32[576,1152]{1,0:T(8,128)S(1)} %fusion.7, bf16[128,8,512]{0,2,1:T(8,128)(2,1)} %bitcast.79, f32[128]{0:T(128)S(1)} %compare_convert_fusion, f32[128,8]{0,1:T(8,128)S(1)} %get-tuple-element.27, f32[1152,128,8]{1,0,2:T(8,128)} %copy-done, pred[128,1152]{0,1:T(8,128)(4,1)} %copy-done.9), kind=kOutput, calls=%fused_computation.17 | convolution fusion | flops 1214449792 | bytes 10637824 | tf_op jit(solution)/shard_map/thk,the->ek/dot_general | solution.py:59
  35.8 0.1 convert.14
  36.0 0.2 bitcast_bitcast_fusion
  36.2 0.1 pad_maximum_fusion
  36.3 25.4 %all_to_all.30 = bf16[8,648,128]{2,1,0:T(8,128)(2,1)S(1)} all-to-all(bf16[8,648,128]{2,1,0:T(8,128)(2,1)S(1)} %pad_maximum_fusion), channel_id=1, replica_groups=mesh['yh'=4,'z'=8,'c'=2,'yl'=2,'x'=4] {'yl','x'}, dimensions={0} | all-to-all | bytes 2654208 | tf_op jit(solution)/shard_map/all_to_all | solution.py:66
  61.7 0.2 reduce_sum.66
  61.9 19.8 %all_to_all.31 = bf16[8,72,128]{2,1,0:T(8,128)(2,1)S(1)} all-to-all(bf16[8,72,128]{2,1,0:T(8,128)(2,1)S(1)} %bitcast.81), channel_id=1, replica_groups=mesh['yh'=4,'z'=8,'c'=2,'yl'=2,'x'=4] {'z'}, dimensions={0} | all-to-all | bytes 294912 | tf_op jit(solution)/shard_map/all_to_all | solution.py:70
  81.8 0.7 broadcast_in_dim.28
  82.4 9.5 %all-to-all-start.3 = ((bf16[8,72,128]{2,1,0:T(8,128)(2,1)}), bf16[8,72,128]{2,1,0:T(8,128)(2,1)S(1)}, u32[]{:S(2)}, u32[]{:S(2)}) async-start(bf16[8,72,128]{2,1,0:T(8,128)(2,1)} %broadcast_in_dim.28), calls=%async_computation.3 | async-start | bytes 294912 | tf_op jit(solution)/shard_map/all_to_all | solution.py:18
  92.0 8.2 %all-to-all-done.3 = bf16[8,72,128]{2,1,0:T(8,128)(2,1)S(1)} async-done(((bf16[8,72,128]{2,1,0:T(8,128)(2,1)}), bf16[8,72,128]{2,1,0:T(8,128)(2,1)S(1)}, u32[]{:S(2)}, u32[]{:S(2)}) %all-to-all-start.3) | async-done | bytes 147488 | tf_op jit(solution)/shard_map/all_to_all | solution.py:18
  100.2 0.7 broadcast_in_dim.30
  100.9 3.4 %all-to-all-start.5 = ((bf16[8,72,128]{2,1,0:T(8,128)(2,1)}), bf16[8,72,128]{2,1,0:T(8,128)(2,1)S(1)}, u32[]{:S(2)}, u32[]{:S(2)}) async-start(bf16[8,72,128]{2,1,0:T(8,128)(2,1)} %broadcast_in_dim.30), calls=%async_computation.5 | async-start | bytes 294912 | tf_op jit(solution)/shard_map/all_to_all | solution.py:18
  104.3 5.4 %all-to-all-done.5 = bf16[8,72,128]{2,1,0:T(8,128)(2,1)S(1)} async-done(((bf16[8,72,128]{2,1,0:T(8,128)(2,1)}), bf16[8,72,128]{2,1,0:T(8,128)(2,1)S(1)}, u32[]{:S(2)}, u32[]{:S(2)}) %all-to-all-start.5) | async-done | bytes 147488 | tf_op jit(solution)/shard_map/all_to_all | solution.py:18
  109.7 0.7 broadcast_in_dim.29
  110.4 3.4 %all-to-all-start.4 = ((bf16[8,72,128]{2,1,0:T(8,128)(2,1)}), bf16[8,72,128]{2,1,0:T(8,128)(2,1)S(1)}, u32[]{:S(2)}, u32[]{:S(2)}) async-start(bf16[8,72,128]{2,1,0:T(8,128)(2,1)} %broadcast_in_dim.29), calls=%async_computation.4 | async-start | bytes 294912 | tf_op jit(solution)/shard_map/all_to_all | solution.py:18
  113.8 3.4 %multiply_convert_fusion = bf16[128,8,576]{0,2,1:T(8,128)(2,1)S(1)} fusion(bf16[128,8,1152]{0,2,1:T(8,128)(2,1)} %copy-done.1, bf16[576,1152]{1,0:T(8,128)(2,1)S(1)} %copy-done.6), kind=kOutput, calls=%fused_computation.19 | convolution fusion | flops 1360134144 | bytes 4866048 | tf_op jit(solution)/shard_map/thk,dk->thd/dot_general | solution.py:51
  117.2 1.4 %copy.46 = bf16[128,4608]{1,0:T(8,128)(2,1)} copy(bf16[128,4608]{0,1:T(8,128)(2,1)S(1)} %bitcast.78) | data formatting | bytes 2359296
  118.6 0.7 bitcast_convert_fusion
  119.3 2.6 %all-to-all-done.4 = bf16[8,72,128]{2,1,0:T(8,128)(2,1)S(1)} async-done(((bf16[8,72,128]{2,1,0:T(8,128)(2,1)}), bf16[8,72,128]{2,1,0:T(8,128)(2,1)S(1)}, u32[]{:S(2)}, u32[]{:S(2)}) %all-to-all-start.4) | async-done | bytes 147488 | tf_op jit(solution)/shard_map/all_to_all | solution.py:18
  121.9 0.7 bitcast_convert_fusion.1
  (17 shorter events, 0.1 us)
Async XLA Ops:
  0.6 8.2 %copy-start.7 = (bf16[128,4096]{1,0:T(8,128)(2,1)S(1)}, bf16[128,4096]{1,0:T(8,128)(2,1)}, u32[]{:S(2)}) copy-start(bf16[128,4096]{1,0:T(8,128)(2,1)} %param.8) | copy-start | bytes 3145732
  2.8 7.3 %copy-start.2 = (bf16[128,4608]{1,0:T(8,128)(2,1)S(1)}, bf16[128,4608]{1,0:T(8,128)(2,1)}, u32[]{:S(2)}) copy-start(bf16[128,4608]{1,0:T(8,128)(2,1)} %param.7) | copy-start | bytes 3538948
  2.8 16.9 %all-to-all-start = ((bf16[8,576,128]{2,1,0:T(8,128)(2,1)}), bf16[8,576,128]{2,1,0:T(8,128)(2,1)S(1)}, u32[]{:S(2)}, u32[]{:S(2)}) async-start(bf16[8,576,128]{2,1,0:T(8,128)(2,1)} %broadcast_in_dim.25), calls=%async_computation | async-start | bytes 2359296 | tf_op jit(solution)/shard_map/all_to_all | solution.py:18
  8.8 2.1 %copy-start.11 = (s32[64]{0:T(128)S(1)}, s32[64]{0:T(128)}, u32[]{:S(2)}) copy-start(s32[64]{0:T(128)} %param.11) | copy-start | bytes 772
  10.9 11.1 %copy-start.3 = (bf16[128,4608]{0,1:T(8,128)(2,1)}, bf16[128,4608]{0,1:T(8,128)(2,1)S(1)}, u32[]{:S(2)}) copy-start(bf16[128,4608]{0,1:T(8,128)(2,1)S(1)} %copy.38) | copy-start | bytes 3538948
  10.9 8.9 %copy-start.10 = (bf16[576,128]{1,0:T(8,128)(2,1)S(1)}, bf16[576,128]{1,0:T(8,128)(2,1)}, u32[]{:S(2)}) copy-start(bf16[576,128]{1,0:T(8,128)(2,1)} %param.10) | copy-start | bytes 442372
  12.3 9.6 %copy-start.9 = (pred[128,1152]{0,1:T(8,128)(4,1)}, pred[128,1152]{0,1:T(8,128)(4,1)S(1)}, u32[]{:S(2)}) copy-start(pred[128,1152]{0,1:T(8,128)(4,1)S(1)} %iota_compare_fusion) | copy-start | bytes 442372
  19.8 4.2 %copy-start.5 = (bf16[576,1152]{1,0:T(8,128)(2,1)}, bf16[576,1152]{1,0:T(8,128)(2,1)S(1)}, u32[]{:S(2)}) copy-start(bf16[576,1152]{1,0:T(8,128)(2,1)S(1)} %constant_dynamic-update-slice_fusion) | copy-start | bytes 3981316
  21.9 2.1 %copy-start = (f32[1152,128,8]{1,0,2:T(8,128)}, f32[1152,128,8]{1,0,2:T(8,128)S(1)}, u32[]{:S(2)}) copy-start(f32[1152,128,8]{1,0,2:T(8,128)S(1)} %convolution_multiply_fusion) | copy-start | bytes 14155780
  21.9 2.1 %copy-start.8 = (bf16[128,4096]{0,1:T(8,128)(2,1)S(1)}, bf16[128,4096]{0,1:T(8,128)(2,1)}, u32[]{:S(2)}) copy-start(bf16[128,4096]{0,1:T(8,128)(2,1)} %copy.52) | copy-start | bytes 3145732
  26.0 2.7 %copy-start.4 = (bf16[128,4608]{0,1:T(8,128)(2,1)S(1)}, bf16[128,4608]{0,1:T(8,128)(2,1)}, u32[]{:S(2)}) copy-start(bf16[128,4608]{0,1:T(8,128)(2,1)} %copy-done.3) | copy-start | bytes 3538948
  27.3 1.4 %copy-start.1 = (bf16[128,8,1152]{0,2,1:T(8,128)(2,1)}, bf16[128,8,1152]{0,2,1:T(8,128)(2,1)S(1)}, u32[]{:S(2)}) copy-start(bf16[128,8,1152]{0,2,1:T(8,128)(2,1)S(1)} %fusion.4) | copy-start | bytes 7077892
  61.7 52.1 %copy-start.6 = (bf16[576,1152]{1,0:T(8,128)(2,1)S(1)}, bf16[576,1152]{1,0:T(8,128)(2,1)}, u32[]{:S(2)}) copy-start(bf16[576,1152]{1,0:T(8,128)(2,1)} %copy-done.5) | copy-start | bytes 3981316
  82.4 17.8 %all-to-all-start.3 = ((bf16[8,72,128]{2,1,0:T(8,128)(2,1)}), bf16[8,72,128]{2,1,0:T(8,128)(2,1)S(1)}, u32[]{:S(2)}, u32[]{:S(2)}) async-start(bf16[8,72,128]{2,1,0:T(8,128)(2,1)} %broadcast_in_dim.28), calls=%async_computation.3 | async-start | bytes 294912 | tf_op jit(solution)/shard_map/all_to_all | solution.py:18
  100.9 8.8 %all-to-all-start.5 = ((bf16[8,72,128]{2,1,0:T(8,128)(2,1)}), bf16[8,72,128]{2,1,0:T(8,128)(2,1)S(1)}, u32[]{:S(2)}, u32[]{:S(2)}) async-start(bf16[8,72,128]{2,1,0:T(8,128)(2,1)} %broadcast_in_dim.30), calls=%async_computation.5 | async-start | bytes 294912 | tf_op jit(solution)/shard_map/all_to_all | solution.py:18
  110.4 11.5 %all-to-all-start.4 = ((bf16[8,72,128]{2,1,0:T(8,128)(2,1)}), bf16[8,72,128]{2,1,0:T(8,128)(2,1)S(1)}, u32[]{:S(2)}, u32[]{:S(2)}) async-start(bf16[8,72,128]{2,1,0:T(8,128)(2,1)} %broadcast_in_dim.29), calls=%async_computation.4 | async-start | bytes 294912 | tf_op jit(solution)/shard_map/all_to_all | solution.py:18

commit v2 on v1

v2 whole, which is shorter than its diff:
```python
import functools

import jax
import jax.numpy as jnp
from jax import lax
from jax.experimental import pallas as pl
from jax.experimental.pallas import tpu as pltpu
from jax.sharding import Mesh
from jax.sharding import PartitionSpec as P

D_LAT = 512
DQK = 576
CLEN = 128
HEADS = 8
KEYS = 1152
PROMPT = 1024
ROWS = CLEN * HEADS
WIDE = 640
PIECE = 80
HS = ("yl", "x")
CTX = ("yh", "z", "c")
ORDER = (0, 2, 1, 3, 4, 6, 5, 7)

score_scale = 192.0 ** (-0.5)
LOG2E = 1.4426950408889634

BF = jnp.bfloat16
F32 = jnp.float32
VM = pl.BlockSpec(memory_space=pltpu.VMEM)
HBM = pl.BlockSpec(memory_space=pl.ANY)
PARAMS = pltpu.CompilerParams(vmem_limit_bytes=56 * 1024 * 1024)
SMALL = pltpu.CompilerParams(vmem_limit_bytes=4 * 1024 * 1024)


def dot(a, b, contract):
    return lax.dot_general(a, b, ((contract[0:1], contract[1:2]), ((), ())), preferred_element_type=F32)


def turn_kernel(q_ref, g_ref, left_ref):
    for i, h in enumerate(ORDER):
        part = q_ref[:, 1152 * (h // 2) + 512 * (h % 2) : 1152 * (h // 2) + 512 * (h % 2) + WIDE]
        turned = part.T
        first = 64 * (h % 2)
        left_ref[:, i * CLEN : (i + 1) * CLEN] = turned[first : first + DQK]
        left_ref[0:D_LAT, ROWS + i * CLEN : ROWS + (i + 1) * CLEN] = g_ref[:, D_LAT * h : D_LAT * (h + 1)].T
    left_ref[D_LAT:DQK, ROWS:] = jnp.zeros((DQK - D_LAT, ROWS), BF)


def turn(queries, grad_out):
    return pl.pallas_call(
        turn_kernel,
        out_shape=jax.ShapeDtypeStruct((DQK, 2 * ROWS), BF),
        in_specs=[VM, VM],
        out_specs=VM,
        compiler_params=PARAMS,
        cost_estimate=pl.CostEstimate(flops=0, bytes_accessed=4600000, transcendentals=0),
    )(queries, grad_out)


def fill_keys(prompt_ref, comp_ref, keys_ref, shift):
    zero = jnp.zeros((WIDE - DQK, KEYS), BF)
    if shift:
        keys_ref[0 : WIDE - DQK] = zero
    else:
        keys_ref[DQK:WIDE] = zero
    for j in range(8):
        keys_ref[shift : shift + DQK, j * CLEN : (j + 1) * CLEN] = prompt_ref[j]
    keys_ref[shift : shift + DQK, PROMPT:KEYS] = comp_ref[...]


def main_kernel(live_ref, q_hbm, g_hbm, left_hbm, prompt_hbm, comp_hbm, terms_hbm, score_grad_hbm, q_ref, g_ref, left_ref, right_ref, terms_ref, even_ref, odd_ref, score_ref, gprob_ref, in_sems, out_sems):
    zero = jnp.zeros((WIDE - DQK, KEYS), BF)
    even_ref[DQK:WIDE] = zero
    odd_ref[0 : WIDE - DQK] = zero

    def keys_in(ref, shift, sem):
        rows = pl.ds(shift, DQK)
        moves = [pltpu.make_async_copy(prompt_hbm.at[j], ref.at[rows, pl.ds(j * CLEN, CLEN)], sem) for j in range(8)]
        return moves + [pltpu.make_async_copy(comp_hbm, ref.at[rows, pl.ds(PROMPT, CLEN)], sem)]

    half_q, half_g = pl.ds(0, 2304), pl.ds(0, 2048)
    rest_q, rest_g = pl.ds(2304, 2304), pl.ds(2048, 2048)
    loads = [
        keys_in(even_ref, 0, in_sems.at[0]),
        [pltpu.make_async_copy(q_hbm.at[:, half_q], q_ref.at[:, half_q], in_sems.at[1])],
        [pltpu.make_async_copy(g_hbm.at[:, half_g], g_ref.at[:, half_g], in_sems.at[2])],
        keys_in(odd_ref, WIDE - DQK, in_sems.at[3]),
        [pltpu.make_async_copy(q_hbm.at[:, rest_q], q_ref.at[:, rest_q], in_sems.at[4])],
        [pltpu.make_async_copy(g_hbm.at[:, rest_g], g_ref.at[:, rest_g], in_sems.at[5])],
        [pltpu.make_async_copy(left_hbm, left_ref, in_sems.at[6])],
    ]
    for load in loads:
        for move in load:
            move.start()

    def arrived(*which):
        for i in which:
            for move in loads[i]:
                move.wait()

    live = live_ref[0]
    pairs = [ORDER[2 * b : 2 * b + 2] for b in range(4)]

    def matmuls(b):
        odd = pairs[b][0] % 2
        starts = [1152 * (h // 2) + 512 * odd for h in pairs[b]]
        q = jnp.concatenate([q_ref[:, s : s + WIDE] for s in starts], axis=0)
        g = jnp.concatenate([g_ref[:, D_LAT * h : D_LAT * (h + 1)] for h in pairs[b]], axis=0)
        keys = odd_ref if odd else even_ref
        first = (WIDE - DQK) * odd
        score_ref[256 * b : 256 * (b + 1)] = dot(q, keys[...], (1, 0))
        gprob_ref[256 * b : 256 * (b + 1)] = dot(g, keys[first : first + D_LAT], (1, 0))

    def softmax(b):
        for r in range(256 * b, 256 * (b + 1), 16):
            slot = r % CLEN + lax.broadcasted_iota(jnp.int32, (16, CLEN), 0)
            own = lax.broadcasted_iota(jnp.int32, (16, CLEN), 1)
            score = score_ref[r : r + 16]
            tail = jnp.where(own <= slot, score[:, PROMPT:], -jnp.inf)
            score = jnp.concatenate([score[:, :PROMPT], tail], axis=1)
            largest = jnp.max(score, axis=1, keepdims=True)
            weight = jnp.exp2((score - largest) * (score_scale * LOG2E))
            total = jnp.sum(weight, axis=1, keepdims=True)
            alive = (slot[:, :1] < live).astype(F32)
            prob = weight * (alive / total)
            gprob = gprob_ref[r : r + 16]
            delta = jnp.sum(prob * gprob, axis=1, keepdims=True)
            right_ref[r : r + 16] = (prob * ((gprob - delta) * score_scale)).astype(BF)
            right_ref[ROWS + r : ROWS + r + 16] = prob.astype(BF)

    outs = []

    def send(source, target, sem):
        outs.append(pltpu.make_async_copy(source, target, sem))
        outs[-1].start()

    arrived(0, 1, 2)
    matmuls(0)
    arrived(3)
    matmuls(1)
    softmax(0)
    arrived(4, 5)
    matmuls(2)
    softmax(1)
    matmuls(3)
    softmax(2)
    softmax(3)
    arrived(6)
    send(right_ref.at[pl.ds(0, ROWS)], score_grad_hbm, out_sems.at[4])
    for n, j in enumerate((PROMPT, 0, 256, 512, 768)):
        wide = min(256, KEYS - j)
        part = dot(left_ref[...], right_ref[:, j : j + wide], (1, 0)).astype(BF)
        if j < PROMPT:
            k = j // CLEN
            terms_ref[k, 0:DQK] = part[:, :CLEN]
            terms_ref[k + 1, 0:DQK] = part[:, CLEN:]
            send(terms_ref.at[pl.ds(k, 2)], terms_hbm.at[pl.ds(k, 2)], out_sems.at[n - 1])
        else:
            for k in range(8):
                rows = min(PIECE, DQK - PIECE * k)
                terms_ref[k, DQK : DQK + rows] = part[PIECE * k : PIECE * k + rows]
                if rows < PIECE:
                    terms_ref[k, DQK + rows : DQK + PIECE] = jnp.zeros((PIECE - rows, CLEN), BF)
    for move in outs:
        move.wait()


def main(live, queries, grad_out, left, prompt, comp):
    return pl.pallas_call(
        main_kernel,
        out_shape=(
            jax.ShapeDtypeStruct((8, DQK + PIECE, CLEN), BF),
            jax.ShapeDtypeStruct((ROWS, KEYS), BF),
        ),
        in_specs=[pl.BlockSpec(memory_space=pltpu.SMEM)] + [HBM] * 5,
        out_specs=(HBM, HBM),
        scratch_shapes=[
            pltpu.VMEM((CLEN, HEADS * DQK), BF),
            pltpu.VMEM((CLEN, HEADS * D_LAT), BF),
            pltpu.VMEM((DQK, 2 * ROWS), BF),
            pltpu.VMEM((2 * ROWS, KEYS), BF),
            pltpu.VMEM((8, DQK + PIECE, CLEN), BF),
            pltpu.VMEM((WIDE, KEYS), BF),
            pltpu.VMEM((WIDE, KEYS), BF),
            pltpu.VMEM((ROWS, KEYS), F32),
            pltpu.VMEM((ROWS, KEYS), F32),
            pltpu.SemaphoreType.DMA((7,)),
            pltpu.SemaphoreType.DMA((5,)),
        ],
        compiler_params=PARAMS,
        cost_estimate=pl.CostEstimate(flops=5200000000, bytes_accessed=12000000, transcendentals=1200000),
    )(live, queries, grad_out, left, prompt, comp)


def query_kernel(grad_ref, prompt_ref, comp_ref, out_ref, token_ref, even_ref, odd_ref):
    @pl.when(pl.program_id(0) == 0)
    def _():
        fill_keys(prompt_ref, comp_ref, even_ref, 0)
        fill_keys(prompt_ref, comp_ref, odd_ref, WIDE - DQK)
        token_ref[...] = jnp.zeros((16, CLEN), BF)

    even = dot(grad_ref[:256], even_ref[...], (1, 1))
    odd = dot(grad_ref[256:], odd_ref[...], (1, 1))
    for i in range(2):
        start = 1152 * i
        e, o = even[128 * i : 128 * (i + 1)], odd[128 * i : 128 * (i + 1)]
        out_ref[:, start : start + 512] = e[:, :512].astype(BF)
        out_ref[:, start + 512 : start + 640] = (e[:, 512:] + o[:, :128]).astype(BF)
        out_ref[:, start + 640 : start + 1152] = o[:, 128:].astype(BF)


def query_grads(score_grad, prompt, comp):
    return pl.pallas_call(
        query_kernel,
        out_shape=(jax.ShapeDtypeStruct((CLEN, HEADS * DQK), BF), jax.ShapeDtypeStruct((16, CLEN), BF)),
        grid=(2,),
        in_specs=[
            pl.BlockSpec((ROWS // 2, KEYS), lambda i: (i, 0)),
            pl.BlockSpec((8, DQK, CLEN), lambda i: (0, 0, 0)),
            pl.BlockSpec((DQK, CLEN), lambda i: (0, 0)),
        ],
        out_specs=(pl.BlockSpec((CLEN, HEADS * DQK // 2), lambda i: (0, i)), pl.BlockSpec((16, CLEN), lambda i: (0, 0))),
        scratch_shapes=[pltpu.VMEM((WIDE, KEYS), BF), pltpu.VMEM((WIDE, KEYS), BF)],
        compiler_params=PARAMS,
        cost_estimate=pl.CostEstimate(flops=1400000000, bytes_accessed=5000000, transcendentals=0),
    )(score_grad, prompt, comp)


def total_of(ref, first, rows):
    total = ref[0, first : first + rows].astype(F32)
    for j in range(1, ref.shape[0]):
        total = total + ref[j, first : first + rows].astype(F32)
    return total


def heads_sum_kernel(terms_ref, token_ref, prompt_ref, comp_ref):
    prompt_ref[0:DQK] = total_of(terms_ref, 0, DQK).astype(BF)
    prompt_ref[DQK:] = jnp.zeros((WIDE - DQK, CLEN), BF)
    comp_ref[...] = total_of(terms_ref, DQK, PIECE).astype(BF)


def heads_sum(terms, token):
    return pl.pallas_call(
        heads_sum_kernel,
        out_shape=(jax.ShapeDtypeStruct((WIDE, CLEN), BF), jax.ShapeDtypeStruct((PIECE, CLEN), BF)),
        in_specs=[VM, VM],
        out_specs=(VM, VM),
        compiler_params=SMALL,
        cost_estimate=pl.CostEstimate(flops=700000, bytes_accessed=1600000, transcendentals=0),
    )(terms, token)


def total_and_join_kernel(high_ref, pieces_ref, mine_ref, other_ref, out_ref, joined_ref):
    total = total_of(pieces_ref, 0, PIECE).astype(BF)
    for j in range(8):
        out_ref[j] = total
    join(high_ref[0], mine_ref, other_ref, joined_ref)


def join(high, mine_ref, other_ref, joined_ref):
    rows = mine_ref.shape[0]

    @pl.when(high == 0)
    def _():
        joined_ref[0:rows] = mine_ref[...].astype(joined_ref.dtype)
        joined_ref[rows:] = other_ref[...].astype(joined_ref.dtype)

    @pl.when(high != 0)
    def _():
        joined_ref[0:rows] = other_ref[...].astype(joined_ref.dtype)
        joined_ref[rows:] = mine_ref[...].astype(joined_ref.dtype)


def total_and_join(high, pieces, mine, other):
    return pl.pallas_call(
        total_and_join_kernel,
        out_shape=(
            jax.ShapeDtypeStruct((8, PIECE, CLEN), BF),
            jax.ShapeDtypeStruct((2 * mine.shape[0], CLEN), BF),
        ),
        in_specs=[pl.BlockSpec(memory_space=pltpu.SMEM), VM, VM, VM],
        out_specs=(VM, VM),
        compiler_params=SMALL,
        cost_estimate=pl.CostEstimate(flops=90000, bytes_accessed=500000, transcendentals=0),
    )(high, pieces, mine, other)


def finish_kernel(high_ref, pieces_ref, mine_ref, other_ref, prompt_ref, comp_ref, joined_ref):
    join(high_ref[0], mine_ref, other_ref, joined_ref)
    comp_ref[...] = joined_ref[0:DQK].astype(F32)
    for j in range(7):
        prompt_ref[PIECE * j : PIECE * (j + 1)] = pieces_ref[j].astype(F32)
    prompt_ref[PIECE * 7 : DQK] = pieces_ref[7, 0 : DQK - PIECE * 7].astype(F32)


def finish(high, pieces, mine, other):
    return pl.pallas_call(
        finish_kernel,
        out_shape=(jax.ShapeDtypeStruct((DQK, CLEN), F32), jax.ShapeDtypeStruct((DQK, CLEN), F32)),
        in_specs=[pl.BlockSpec(memory_space=pltpu.SMEM), VM, VM, VM],
        out_specs=(VM, VM),
        scratch_shapes=[pltpu.VMEM((WIDE, CLEN), BF)],
        compiler_params=SMALL,
        cost_estimate=pl.CostEstimate(flops=90000, bytes_accessed=900000, transcendentals=0),
    )(high, pieces, mine, other)


def swap(block, axis, count, bit):
    return lax.ppermute(block, axis, [(i, i ^ bit) for i in range(count)])


def on_device(queries, grad_out, prompt_kv, comp_kv, lengths):
    sample = lax.axis_index(CTX)
    live = lax.dynamic_slice(lengths, (sample,), (1,))
    prompt = lax.all_to_all(jnp.broadcast_to(prompt_kv[None], (8,) + prompt_kv.shape), HS, 0, 0)
    left = turn(queries, grad_out)
    terms, score_grad = main(live, queries, grad_out, left, prompt, comp_kv)
    terms = lax.all_to_all(terms, HS, 0, 0)
    grad_queries, token = query_grads(score_grad, prompt, comp_kv)
    prompt_part, comp = heads_sum(terms, token)
    x, yl = lax.axis_index("x"), lax.axis_index("yl")
    high = [(x & 1).reshape(1), (x >> 1).reshape(1), yl.reshape(1)]
    pieces = lax.all_to_all(prompt_part.reshape(8, PIECE, CLEN), "z", 0, 0)
    pieces, comp = total_and_join(high[0], pieces, comp, swap(comp, "x", 4, 1))
    pieces = lax.all_to_all(pieces, ("yh", "c"), 0, 0)
    pieces, comp = total_and_join(high[1], pieces, comp, swap(comp, "x", 4, 2))
    pieces = lax.all_to_all(pieces, "z", 0, 0)
    grad_prompt, grad_comp = finish(high[2], pieces, comp, swap(comp, "yl", 2, 1))
    return (grad_queries, grad_prompt, grad_comp)


def solution(mesh):
    parts = Mesh(mesh.devices.reshape(4, 8, 2, 2, 4), CTX + HS)
    in_specs = (P(CTX, HS), P(CTX, HS), P(None, HS), P(None, CTX), P())
    out_specs = (P(CTX, HS), P(None, HS), P(None, CTX))
    return jax.shard_map(
        on_device, mesh=parts, in_specs=in_specs, out_specs=out_specs, check_vma=False
    )
```

time: 124 us -> 112 us (0.903)
  blocking collectives: 45.2 us -> 0 us
  Pallas kernels: 0 us -> 23.9 us
  starting transfers between devices: 22.3 us -> 45.5 us
  matrix products: 14.4 us -> 0 us
  waiting for transfers between devices: 23.6 us -> 36.6 us
  other arithmetic: 5.96 us -> 0 us
  local copies, waits for them, and re-layouts: 10.3 us -> 4.4 us
    all_to_all x2 -> x0, blocking collectives: 45.2 us -> none  [the longest x1 25.4 us: on_device(): terms = lax.all_to_all(terms, HS, 0, 0)]
    pallas_call x0 -> x7, Pallas kernels: none -> 23.9 us  [the longest x1 11.7 us: main(): pl.pallas_call(main_kernel, out_shape=(jax.ShapeDtypeStruct((8, DQK + PIE...]
    all_to_all x4 -> x5, starting transfers between devices: 22.3 us -> 37.5 us  [the longest x1 10.8 us: on_device(): pieces = lax.all_to_all(prompt_part.reshape(8, PIECE, CLEN), 'z', 0, 0)]
    dot_general x5 -> x0, matrix products: 14.4 us -> none  [the longest x1 5.35 us: on_device(): jnp.einsum('thk,the->ek', kept_probs, cotangent, preferred_element_type=j...]
    ppermute x0 -> x3, waiting for transfers between devices: none -> 8.32 us  [swap(): return lax.ppermute(block, axis, [(i, i ^ bit) for i in range(count)])]
    ppermute x0 -> x3, starting transfers between devices: none -> 8.05 us  [swap(): return lax.ppermute(block, axis, [(i, i ^ bit) for i in range(count)])]
    all_to_all x4 -> x5, waiting for transfers between devices: 23.6 us -> 28.2 us  [the longest x1 12.7 us: on_device(): terms = lax.all_to_all(terms, HS, 0, 0)]
    convert_element_type x4 -> x0, other arithmetic: 3.36 us -> none  [the longest x1 1.23 us: on_device(): grad_score = (live_prob * (grad_prob - row_delta)).astype(jnp.bfloat16)]
  transfers between devices with their start and end apart: 4 -> 8, of which waited for: 4 -> 8; matrix products, arithmetic and copies ran while one was open for 7% -> 1% of each run, Pallas kernels for 0% -> 8%
where the time goes in v2:
time: 112 us; the launch traced here: 111 us
  starting transfers between devices  45.5 us (41%)
  waiting for transfers between devices  36.6 us (33%)
  Pallas kernels  23.9 us (21%)
  local copies, waits for them, and re-layouts  4.4 us (4%)
    all_to_all x1, waiting for transfers between devices, on_device(): terms = lax.all_to_all(terms, HS, 0, 0)  12.7 us
    pallas_call x1, Pallas kernels, main(): pl.pallas_call(main_kernel, out_shape=(jax.ShapeDtypeStruct((8, DQK + PIE...  11.7 us
    all_to_all x1, starting transfers between devices, on_device(): pieces = lax.all_to_all(prompt_part.reshape(8, PIECE, CLEN), 'z', 0, 0)  10.8 us
    all_to_all x1, starting transfers between devices, on_device(): pieces = lax.all_to_all(pieces, ('yh', 'c'), 0, 0)  8.83 us
    all_to_all x1, starting transfers between devices, on_device(): terms = lax.all_to_all(terms, HS, 0, 0)  8.41 us
    ppermute x3, waiting for transfers between devices, swap(): return lax.ppermute(block, axis, [(i, i ^ bit) for i in range(count)])  8.32 us
    ppermute x3, starting transfers between devices, swap(): return lax.ppermute(block, axis, [(i, i ^ bit) for i in range(count)])  8.05 us
    all_to_all x1, waiting for transfers between devices, on_device(): lax.all_to_all(jnp.broadcast_to(prompt_kv[None], (8,) + prompt_kv.shape),...  6.51 us
  transfers between devices with their start and end apart: 8, of which 8 were waited for; matrix products, arithmetic and copies ran while one was open for 1% of the time, Pallas kernels for 8%

profile of v2, /device:TPU:1, one launch (start us, length us, event | category | flops | bytes accessed | tf_op | source)
XLA Modules:
  0.0 111.1 jit_solution(8485625396856170688)
XLA Ops:
  0.6 2.1 %broadcast_in_dim.2 = bf16[8,576,128]{2,1,0:T(8,128)(2,1)} broadcast(bf16[576,128]{1,0:T(8,128)(2,1)} %param.7), dimensions={1,2} | broadcast | bytes 1327104 | tf_op jit(solution)/shard_map/broadcast_in_dim | solution.py:315
  2.7 0.0 copy-start.2
  2.7 6.0 %all-to-all-start = ((bf16[8,576,128]{2,1,0:T(8,128)(2,1)}), bf16[8,576,128]{2,1,0:T(8,128)(2,1)S(1)}, u32[]{:S(2)}, u32[]{:S(2)}) async-start(bf16[8,576,128]{2,1,0:T(8,128)(2,1)} %broadcast_in_dim.2), calls=%async_computation | async-start | bytes 2359296 | tf_op jit(solution)/shard_map/all_to_all | solution.py:315
  8.7 0.0 copy-done.2
  8.7 0.6 dynamic_slice.3.live_ref
  9.3 3.8 %shard_map.76.left_hbm = bf16[576,2048]{1,0:T(8,128)(2,1)} custom-call(bf16[128,4608]{1,0:T(8,128)(2,1)} %q_hbm.1, bf16[128,4096]{1,0:T(8,128)(2,1)} %g_hbm.1), custom_call_target="tpu_custom_call" | custom-call | bytes 4600000 | tf_op jit(solution)/shard_map/pallas_call | solution.py:50
  13.0 6.5 %all-to-all-done.prompt_hbm.prompt_ref = bf16[8,576,128]{2,1,0:T(8,128)(2,1)S(1)} async-done(((bf16[8,576,128]{2,1,0:T(8,128)(2,1)}), bf16[8,576,128]{2,1,0:T(8,128)(2,1)S(1)}, u32[]{:S(2)}, u32[]{:S(2)}) %all-to-all-start) | async-done | bytes 1179680 | tf_op jit(solution)/shard_map/all_to_all | solution.py:315
  19.6 0.0 copy-start.1
  19.6 1.0 copy-done.1
  20.6 11.7 %shard_map.77 = (bf16[8,656,128]{2,1,0:T(8,128)(2,1)}, bf16[1024,1152]{1,0:T(8,128)(2,1)}) custom-call(s32[1]{0:T(128)} %dynamic_slice.3.live_ref, bf16[128,4608]{1,0:T(8,128)(2,1)} %q_hbm.1, bf16[128,4096]{1,0:T(8,128)(2,1)} %g_hbm.1, bf16[576,2048]{1,0:T(8,128)(2,1)} %shard_map.76.left_hbm, bf16[8,576,128]{2,1,0:T(8,128)(2,1)} %copy-done.1, ...), custom_call_target="tpu_custom_call" | custom-call | flops 5200000000 | bytes 12000000 | tf_op jit(solution)/shard_map/pallas_call | solution.py:169
  32.3 8.4 %all-to-all-start.1 = ((bf16[8,656,128]{2,1,0:T(8,128)(2,1)}), bf16[8,656,128]{2,1,0:T(8,128)(2,1)S(1)}, u32[]{:S(2)}, u32[]{:S(2)}) async-start(bf16[8,656,128]{2,1,0:T(8,128)(2,1)} %get-tuple-element.17), calls=%async_computation.1 | async-start | bytes 2686976 | tf_op jit(solution)/shard_map/all_to_all | solution.py:318
  40.8 5.4 %shard_map.78 = (bf16[128,4608]{1,0:T(8,128)(2,1)}, bf16[16,128]{1,0:T(8,128)(2,1)}) custom-call(bf16[1024,1152]{1,0:T(8,128)(2,1)} %get-tuple-element.15.grad_ref, bf16[8,576,128]{2,1,0:T(8,128)(2,1)} %copy-done.1, bf16[576,128]{1,0:T(8,128)(2,1)} %comp_ref.1), custom_call_target="tpu_custom_call" | custom-call | flops 1400000000 | bytes 5000000 | tf_op jit(solution)/shard_map/pallas_call | solution.py:213
  46.1 12.7 %all-to-all-done.1.terms_ref = bf16[8,656,128]{2,1,0:T(8,128)(2,1)S(1)} async-done(((bf16[8,656,128]{2,1,0:T(8,128)(2,1)}), bf16[8,656,128]{2,1,0:T(8,128)(2,1)S(1)}, u32[]{:S(2)}, u32[]{:S(2)}) %all-to-all-start.1) | async-done | bytes 1343520 | tf_op jit(solution)/shard_map/all_to_all | solution.py:318
  58.8 0.0 copy-start
  58.8 0.7 copy-done
  59.5 0.8 shard_map.79
  60.3 10.8 %all-to-all-start.2 = ((bf16[8,80,128]{2,1,0:T(8,128)(2,1)}), bf16[8,80,128]{2,1,0:T(8,128)(2,1)S(1)}, u32[]{:S(2)}, u32[]{:S(2)}) async-start(bf16[8,80,128]{2,1,0:T(8,128)(2,1)} %bitcast.3), calls=%async_computation.2 | async-start | bytes 327680 | tf_op jit(solution)/shard_map/all_to_all | solution.py:323
  71.2 1.9 %collective-permute-start = (bf16[80,128]{1,0:T(8,128)(2,1)S(1)}, bf16[80,128]{1,0:T(8,128)(2,1)S(1)}, u32[]{:S(2)}, u32[]{:S(2)}) collective-permute-start(bf16[80,128]{1,0:T(8,128)(2,1)S(1)} %get-tuple-element.20.mine_ref), channel_id=1, source_target_pairs={{0,1},{1,0},{2,3},{3,2},{4,5},{5,4},{6,7},{7,6},{8,9},{9,8},{10,11... | collective-permute-start | bytes 61448 | tf_op jit(solution)/shard_map/ppermute | solution.py:309
  73.1 2.8 %collective-permute-done.other_ref = bf16[80,128]{1,0:T(8,128)(2,1)S(1)} collective-permute-done((bf16[80,128]{1,0:T(8,128)(2,1)S(1)}, bf16[80,128]{1,0:T(8,128)(2,1)S(1)}, u32[]{:S(2)}, u32[]{:S(2)}) %collective-permute-start) | collective-permute-done | bytes 20512 | tf_op jit(solution)/shard_map/ppermute | solution.py:309
  75.8 3.4 %all-to-all-done.2.pieces_ref = bf16[8,80,128]{2,1,0:T(8,128)(2,1)S(1)} async-done(((bf16[8,80,128]{2,1,0:T(8,128)(2,1)}), bf16[8,80,128]{2,1,0:T(8,128)(2,1)S(1)}, u32[]{:S(2)}, u32[]{:S(2)}) %all-to-all-start.2) | async-done | bytes 163872 | tf_op jit(solution)/shard_map/all_to_all | solution.py:323
  79.2 0.7 shard_map.80
  79.9 8.8 %all-to-all-start.3 = ((bf16[8,80,128]{2,1,0:T(8,128)(2,1)}), bf16[8,80,128]{2,1,0:T(8,128)(2,1)S(1)}, u32[]{:S(2)}, u32[]{:S(2)}) async-start(bf16[8,80,128]{2,1,0:T(8,128)(2,1)} %get-tuple-element.21), calls=%async_computation.3 | async-start | bytes 327680 | tf_op jit(solution)/shard_map/all_to_all | solution.py:325
  88.8 3.3 %collective-permute-start.1 = (bf16[160,128]{1,0:T(8,128)(2,1)S(1)}, bf16[160,128]{1,0:T(8,128)(2,1)S(1)}, u32[]{:S(2)}, u32[]{:S(2)}) collective-permute-start(bf16[160,128]{1,0:T(8,128)(2,1)S(1)} %get-tuple-element.22.mine_ref), channel_id=1, source_target_pairs={{0,2},{1,3},{2,0},{3,1},{4,6},{5,7},{6,4},{7,5},{8,10},{9,11},{10,... | collective-permute-start | bytes 122888 | tf_op jit(solution)/shard_map/ppermute | solution.py:309
  92.1 3.2 %collective-permute-done.1.other_ref = bf16[160,128]{1,0:T(8,128)(2,1)S(1)} collective-permute-done((bf16[160,128]{1,0:T(8,128)(2,1)S(1)}, bf16[160,128]{1,0:T(8,128)(2,1)S(1)}, u32[]{:S(2)}, u32[]{:S(2)}) %collective-permute-start.1) | collective-permute-done | bytes 40992 | tf_op jit(solution)/shard_map/ppermute | solution.py:309
  95.3 2.7 %all-to-all-done.3.pieces_ref = bf16[8,80,128]{2,1,0:T(8,128)(2,1)S(1)} async-done(((bf16[8,80,128]{2,1,0:T(8,128)(2,1)}), bf16[8,80,128]{2,1,0:T(8,128)(2,1)S(1)}, u32[]{:S(2)}, u32[]{:S(2)}) %all-to-all-start.3) | async-done | bytes 163872 | tf_op jit(solution)/shard_map/all_to_all | solution.py:325
  98.0 0.7 shard_map.81
  98.7 3.4 %all-to-all-start.4 = ((bf16[8,80,128]{2,1,0:T(8,128)(2,1)}), bf16[8,80,128]{2,1,0:T(8,128)(2,1)S(1)}, u32[]{:S(2)}, u32[]{:S(2)}) async-start(bf16[8,80,128]{2,1,0:T(8,128)(2,1)} %get-tuple-element.23), calls=%async_computation.4 | async-start | bytes 327680 | tf_op jit(solution)/shard_map/all_to_all | solution.py:327
  102.1 2.9 %collective-permute-start.2 = (bf16[320,128]{1,0:T(8,128)(2,1)S(1)}, bf16[320,128]{1,0:T(8,128)(2,1)S(1)}, u32[]{:S(2)}, u32[]{:S(2)}) collective-permute-start(bf16[320,128]{1,0:T(8,128)(2,1)S(1)} %get-tuple-element.24.mine_ref), channel_id=1, source_target_pairs={{0,4},{4,0},{1,5},{5,1},{2,6},{6,2},{3,7},{7,3},{8,12},{12,8},{9,1... | collective-permute-start | bytes 245768 | tf_op jit(solution)/shard_map/ppermute | solution.py:309
  104.9 2.3 %collective-permute-done.2.other_ref = bf16[320,128]{1,0:T(8,128)(2,1)S(1)} collective-permute-done((bf16[320,128]{1,0:T(8,128)(2,1)S(1)}, bf16[320,128]{1,0:T(8,128)(2,1)S(1)}, u32[]{:S(2)}, u32[]{:S(2)}) %collective-permute-start.2) | collective-permute-done | bytes 81952 | tf_op jit(solution)/shard_map/ppermute | solution.py:309
  107.3 3.0 %all-to-all-done.4.pieces_ref = bf16[8,80,128]{2,1,0:T(8,128)(2,1)S(1)} async-done(((bf16[8,80,128]{2,1,0:T(8,128)(2,1)}), bf16[8,80,128]{2,1,0:T(8,128)(2,1)S(1)}, u32[]{:S(2)}, u32[]{:S(2)}) %all-to-all-start.4) | async-done | bytes 163872 | tf_op jit(solution)/shard_map/all_to_all | solution.py:327
  110.2 0.8 shard_map.82
Async XLA Ops:
  2.7 6.0 %copy-start.2 = (s32[64]{0:T(128)S(1)}, s32[64]{0:T(128)}, u32[]{:S(2)}) copy-start(s32[64]{0:T(128)} %param.9) | copy-start | bytes 772
  2.7 16.9 %all-to-all-start = ((bf16[8,576,128]{2,1,0:T(8,128)(2,1)}), bf16[8,576,128]{2,1,0:T(8,128)(2,1)S(1)}, u32[]{:S(2)}, u32[]{:S(2)}) async-start(bf16[8,576,128]{2,1,0:T(8,128)(2,1)} %broadcast_in_dim.2), calls=%async_computation | async-start | bytes 2359296 | tf_op jit(solution)/shard_map/all_to_all | solution.py:315
  19.6 1.1 copy-start.1
  32.3 26.5 %all-to-all-start.1 = ((bf16[8,656,128]{2,1,0:T(8,128)(2,1)}), bf16[8,656,128]{2,1,0:T(8,128)(2,1)S(1)}, u32[]{:S(2)}, u32[]{:S(2)}) async-start(bf16[8,656,128]{2,1,0:T(8,128)(2,1)} %get-tuple-element.17), calls=%async_computation.1 | async-start | bytes 2686976 | tf_op jit(solution)/shard_map/all_to_all | solution.py:318
  58.8 0.7 copy-start
  60.3 18.9 %all-to-all-start.2 = ((bf16[8,80,128]{2,1,0:T(8,128)(2,1)}), bf16[8,80,128]{2,1,0:T(8,128)(2,1)S(1)}, u32[]{:S(2)}, u32[]{:S(2)}) async-start(bf16[8,80,128]{2,1,0:T(8,128)(2,1)} %bitcast.3), calls=%async_computation.2 | async-start | bytes 327680 | tf_op jit(solution)/shard_map/all_to_all | solution.py:323
  71.2 4.7 %collective-permute-start = (bf16[80,128]{1,0:T(8,128)(2,1)S(1)}, bf16[80,128]{1,0:T(8,128)(2,1)S(1)}, u32[]{:S(2)}, u32[]{:S(2)}) collective-permute-start(bf16[80,128]{1,0:T(8,128)(2,1)S(1)} %get-tuple-element.20.mine_ref), channel_id=1, source_target_pairs={{0,1},{1,0},{2,3},{3,2},{4,5},{5,4},{6,7},{7,6},{8,9},{9,8},{10,11... | collective-permute-start | bytes 61448 | tf_op jit(solution)/shard_map/ppermute | solution.py:309
  79.9 18.0 %all-to-all-start.3 = ((bf16[8,80,128]{2,1,0:T(8,128)(2,1)}), bf16[8,80,128]{2,1,0:T(8,128)(2,1)S(1)}, u32[]{:S(2)}, u32[]{:S(2)}) async-start(bf16[8,80,128]{2,1,0:T(8,128)(2,1)} %get-tuple-element.21), calls=%async_computation.3 | async-start | bytes 327680 | tf_op jit(solution)/shard_map/all_to_all | solution.py:325
  88.8 6.5 %collective-permute-start.1 = (bf16[160,128]{1,0:T(8,128)(2,1)S(1)}, bf16[160,128]{1,0:T(8,128)(2,1)S(1)}, u32[]{:S(2)}, u32[]{:S(2)}) collective-permute-start(bf16[160,128]{1,0:T(8,128)(2,1)S(1)} %get-tuple-element.22.mine_ref), channel_id=1, source_target_pairs={{0,2},{1,3},{2,0},{3,1},{4,6},{5,7},{6,4},{7,5},{8,10},{9,11},{10,... | collective-permute-start | bytes 122888 | tf_op jit(solution)/shard_map/ppermute | solution.py:309
  98.7 11.6 %all-to-all-start.4 = ((bf16[8,80,128]{2,1,0:T(8,128)(2,1)}), bf16[8,80,128]{2,1,0:T(8,128)(2,1)S(1)}, u32[]{:S(2)}, u32[]{:S(2)}) async-start(bf16[8,80,128]{2,1,0:T(8,128)(2,1)} %get-tuple-element.23), calls=%async_computation.4 | async-start | bytes 327680 | tf_op jit(solution)/shard_map/all_to_all | solution.py:327
  102.1 5.2 %collective-permute-start.2 = (bf16[320,128]{1,0:T(8,128)(2,1)S(1)}, bf16[320,128]{1,0:T(8,128)(2,1)S(1)}, u32[]{:S(2)}, u32[]{:S(2)}) collective-permute-start(bf16[320,128]{1,0:T(8,128)(2,1)S(1)} %get-tuple-element.24.mine_ref), channel_id=1, source_target_pairs={{0,4},{4,0},{1,5},{5,1},{2,6},{6,2},{3,7},{7,3},{8,12},{12,8},{9,1... | collective-permute-start | bytes 245768 | tf_op jit(solution)/shard_map/ppermute | solution.py:309

commit v3 on v2

v3 whole, which is shorter than its diff:
```python
import functools

import jax
import jax.numpy as jnp
from jax import lax
from jax.experimental import pallas as pl
from jax.experimental.pallas import tpu as pltpu
from jax.sharding import Mesh
from jax.sharding import PartitionSpec as P

D_LAT = 512
DQK = 576
CLEN = 128
HEADS = 8
KEYS = 1152
PROMPT = 1024
ROWS = CLEN * HEADS
WIDE = 640
PIECE = 80
EDGE = 64
HALF = 288
SLICE = 48
KEYS_AT = 1024
TALL = 9216
HS = ("yl", "x")
CTX = ("yh", "z", "c")
ORDER = (0, 2, 1, 3, 4, 6, 5, 7)

score_scale = 192.0 ** (-0.5)
LOG2E = 1.4426950408889634

BF = jnp.bfloat16
F32 = jnp.float32
VM = pl.BlockSpec(memory_space=pltpu.VMEM)
HBM = pl.BlockSpec(memory_space=pl.ANY)
PARAMS = pltpu.CompilerParams(vmem_limit_bytes=44 * 1024 * 1024)
SMALL = pltpu.CompilerParams(vmem_limit_bytes=4 * 1024 * 1024)


def dot(a, b, contract):
    return lax.dot_general(a, b, ((contract[0:1], contract[1:2]), ((), ())), preferred_element_type=F32)


def turn_kernel(q_ref, g_ref, left_ref):
    for i, h in enumerate(ORDER):
        part = q_ref[:, 1152 * (h // 2) + 512 * (h % 2) : 1152 * (h // 2) + 512 * (h % 2) + WIDE]
        turned = part.T
        first = 64 * (h % 2)
        left_ref[:, i * CLEN : (i + 1) * CLEN] = turned[first : first + DQK]
        left_ref[0:D_LAT, ROWS + i * CLEN : ROWS + (i + 1) * CLEN] = g_ref[:, D_LAT * h : D_LAT * (h + 1)].T
    left_ref[D_LAT:DQK, ROWS:] = jnp.zeros((DQK - D_LAT, ROWS), BF)


def turn(queries, grad_out):
    return pl.pallas_call(
        turn_kernel,
        out_shape=jax.ShapeDtypeStruct((DQK, 2 * ROWS), BF),
        in_specs=[VM, VM],
        out_specs=VM,
        compiler_params=PARAMS,
        cost_estimate=pl.CostEstimate(flops=0, bytes_accessed=4600000, transcendentals=0),
    )(queries, grad_out)


def after_kernel(block_ref, done_ref, out_ref):
    del block_ref, done_ref, out_ref


def after(block, done):
    return pl.pallas_call(
        after_kernel,
        out_shape=jax.ShapeDtypeStruct(block.shape, block.dtype),
        in_specs=[HBM, HBM],
        out_specs=HBM,
        input_output_aliases={0: 0},
        compiler_params=SMALL,
        cost_estimate=pl.CostEstimate(flops=0, bytes_accessed=0, transcendentals=0),
    )(block, done)


def main_kernel(lengths_ref, q_ref, g_ref, left_ref, mine_ref, other_ref, comp_ref, send_ref, keep_ref, tall_hbm, right_ref, keys_ref, score_ref, gprob_ref, sems):
    live, core = lengths_ref[lax.axis_index(CTX)], lax.axis_index("c")
    zero = jnp.zeros((EDGE, KEYS), BF)
    keys_ref[0:EDGE] = zero
    keys_ref[EDGE + DQK :] = zero
    for ref, half in ((mine_ref, core), (other_ref, 1 - core)):
        rows = pl.ds(pl.multiple_of(EDGE + HALF * half, 16), HALF)
        for j in range(8):
            keys_ref[rows, j * CLEN : (j + 1) * CLEN] = ref[j]
    keys_ref[EDGE : EDGE + DQK, PROMPT:] = comp_ref[...]
    pairs = [ORDER[2 * b : 2 * b + 2] for b in range(4)]

    def matmuls(b):
        odd = pairs[b][0] % 2
        starts = [1152 * (h // 2) + 512 * odd for h in pairs[b]]
        q = jnp.concatenate([q_ref[:, s : s + WIDE] for s in starts], axis=0)
        g = jnp.concatenate([g_ref[:, D_LAT * h : D_LAT * (h + 1)] for h in pairs[b]], axis=0)
        first = EDGE * (1 - odd)
        score_ref[256 * b : 256 * (b + 1)] = dot(q, keys_ref[first : first + WIDE], (1, 0))
        gprob_ref[256 * b : 256 * (b + 1)] = dot(g, keys_ref[EDGE : EDGE + D_LAT], (1, 0))

    def softmax(b):
        for r in range(256 * b, 256 * (b + 1), 16):
            slot = r % CLEN + lax.broadcasted_iota(jnp.int32, (16, CLEN), 0)
            own = lax.broadcasted_iota(jnp.int32, (16, CLEN), 1)
            score = score_ref[r : r + 16]
            tail = jnp.where(own <= slot, score[:, PROMPT:], -jnp.inf)
            score = jnp.concatenate([score[:, :PROMPT], tail], axis=1)
            largest = jnp.max(score, axis=1, keepdims=True)
            weight = jnp.exp2((score - largest) * (score_scale * LOG2E))
            total = jnp.sum(weight, axis=1, keepdims=True)
            alive = (slot[:, :1] < live).astype(F32)
            prob = weight * (alive / total)
            gprob = gprob_ref[r : r + 16]
            delta = jnp.sum(prob * gprob, axis=1, keepdims=True)
            right_ref[r : r + 16] = (prob * ((gprob - delta) * score_scale)).astype(BF)
            right_ref[ROWS + r : ROWS + r + 16] = prob.astype(BF)

    outs = []

    def send(source, target, sem):
        outs.append(pltpu.make_async_copy(source, target, sem))
        outs[-1].start()

    send(keys_ref, tall_hbm.at[pl.ds(KEYS_AT, DQK + 2 * EDGE)], sems.at[0])
    matmuls(0)
    matmuls(1)
    softmax(0)
    matmuls(2)
    softmax(1)
    matmuls(3)
    softmax(2)
    softmax(3)
    send(right_ref.at[pl.ds(0, ROWS)], tall_hbm.at[pl.ds(0, ROWS)], sems.at[1])
    for j in range(0, PROMPT, 256):
        part = dot(left_ref[...], right_ref[:, j : j + 256], (1, 0)).astype(BF)
        for k in range(2):
            top, low = part[:HALF, CLEN * k : CLEN * (k + 1)], part[HALF:, CLEN * k : CLEN * (k + 1)]
            send_ref[j // CLEN + k] = jnp.where(core == 0, low, top)
            keep_ref[j // CLEN + k, 0:HALF] = jnp.where(core == 0, top, low)
    part = dot(left_ref[...], right_ref[:, PROMPT:], (1, 0)).astype(BF)
    for k in range(8):
        rows = min(PIECE, DQK - PIECE * k)
        keep_ref[k, HALF : HALF + rows] = part[PIECE * k : PIECE * k + rows]
        if rows < PIECE:
            keep_ref[k, HALF + rows :] = jnp.zeros((PIECE - rows, CLEN), BF)
    for move in outs:
        move.wait()


def main(lengths, queries, grad_out, left, mine, other, comp):
    return pl.pallas_call(
        main_kernel,
        out_shape=(
            jax.ShapeDtypeStruct((8, HALF, CLEN), BF),
            jax.ShapeDtypeStruct((8, HALF + PIECE, CLEN), BF),
            jax.ShapeDtypeStruct((TALL, KEYS), BF),
        ),
        in_specs=[pl.BlockSpec(memory_space=pltpu.SMEM)] + [VM] * 6,
        out_specs=(VM, VM, HBM),
        scratch_shapes=[
            pltpu.VMEM((2 * ROWS, KEYS), BF),
            pltpu.VMEM((DQK + 2 * EDGE, KEYS), BF),
            pltpu.VMEM((ROWS, KEYS), F32),
            pltpu.VMEM((ROWS, KEYS), F32),
            pltpu.SemaphoreType.DMA((2,)),
        ],
        compiler_params=PARAMS,
        cost_estimate=pl.CostEstimate(flops=5200000000, bytes_accessed=12000000, transcendentals=1200000),
    )(lengths, queries, grad_out, left, mine, other, comp)


def query_kernel(tall_hbm, out_hbm, same_hbm, grad_ref, keys_ref, out_ref, in_sems, out_sems):
    del same_hbm
    loads = [pltpu.make_async_copy(tall_hbm.at[pl.ds(KEYS_AT, DQK + 2 * EDGE)], keys_ref, in_sems.at[2])]
    for b in range(2):
        rows = pl.ds(512 * b, 512)
        loads.append(pltpu.make_async_copy(tall_hbm.at[rows], grad_ref.at[rows], in_sems.at[b]))
    for load in loads:
        load.start()
    loads[0].wait()
    outs = []
    for b in range(2):
        loads[b + 1].wait()
        even = dot(grad_ref[512 * b : 512 * b + 256], keys_ref[EDGE:], (1, 1))
        odd = dot(grad_ref[512 * b + 256 : 512 * b + 512], keys_ref[:WIDE], (1, 1))
        for i in range(2):
            start = 1152 * (2 * b + i)
            e, o = even[128 * i : 128 * (i + 1)], odd[128 * i : 128 * (i + 1)]
            out_ref[:, start : start + 512] = e[:, :512].astype(BF)
            out_ref[:, start + 512 : start + 640] = (e[:, 512:] + o[:, :128]).astype(BF)
            out_ref[:, start + 640 : start + 1152] = o[:, 128:].astype(BF)
        columns = pl.ds(2304 * b, 2304)
        outs.append(pltpu.make_async_copy(out_ref.at[:, columns], out_hbm.at[:, columns], out_sems.at[b]))
        outs[-1].start()
    for move in outs:
        move.wait()


def query_grads(tall):
    return pl.pallas_call(
        query_kernel,
        out_shape=(jax.ShapeDtypeStruct((CLEN, HEADS * DQK), BF), jax.ShapeDtypeStruct(tall.shape, BF)),
        in_specs=[HBM],
        out_specs=(HBM, HBM),
        input_output_aliases={0: 1},
        scratch_shapes=[
            pltpu.VMEM((ROWS, KEYS), BF),
            pltpu.VMEM((DQK + 2 * EDGE, KEYS), BF),
            pltpu.VMEM((CLEN, HEADS * DQK), BF),
            pltpu.SemaphoreType.DMA((3,)),
            pltpu.SemaphoreType.DMA((2,)),
        ],
        compiler_params=PARAMS,
        cost_estimate=pl.CostEstimate(flops=1400000000, bytes_accessed=5000000, transcendentals=0),
    )(tall)


def cores_sum_kernel(keep_ref, got_ref, out_ref):
    for j in range(8):
        out_ref[j, 0:HALF] = (keep_ref[j, 0:HALF].astype(F32) + got_ref[j].astype(F32)).astype(BF)
        out_ref[j, HALF:] = keep_ref[j, HALF:]


def cores_sum(keep, got):
    return pl.pallas_call(
        cores_sum_kernel,
        out_shape=jax.ShapeDtypeStruct(keep.shape, BF),
        in_specs=[VM, VM],
        out_specs=VM,
        compiler_params=SMALL,
        cost_estimate=pl.CostEstimate(flops=300000, bytes_accessed=2100000, transcendentals=0),
    )(keep, got)


def total_of(ref, first, rows):
    total = ref[0, first : first + rows].astype(F32)
    for j in range(1, ref.shape[0]):
        total = total + ref[j, first : first + rows].astype(F32)
    return total


def heads_sum_kernel(terms_ref, tall_hbm, prompt_ref, comp_ref):
    del tall_hbm
    prompt_ref[0:HALF] = total_of(terms_ref, 0, HALF).astype(BF)
    prompt_ref[HALF:] = jnp.zeros((8 * SLICE - HALF, CLEN), BF)
    comp_ref[...] = total_of(terms_ref, HALF, PIECE).astype(BF)


def heads_sum(terms, tall):
    return pl.pallas_call(
        heads_sum_kernel,
        out_shape=(jax.ShapeDtypeStruct((8 * SLICE, CLEN), BF), jax.ShapeDtypeStruct((PIECE, CLEN), BF)),
        in_specs=[VM, HBM],
        out_specs=(VM, VM),
        compiler_params=PARAMS,
        cost_estimate=pl.CostEstimate(flops=400000, bytes_accessed=900000, transcendentals=0),
    )(terms, tall)


def join(bit, mine_ref, other_ref, joined_ref):
    axis, value = (("x", 1), ("x", 2), ("yl", 1))[bit]
    high = lax.axis_index(axis) & value
    rows = mine_ref.shape[0]
    mine, other = mine_ref[...].astype(joined_ref.dtype), other_ref[...].astype(joined_ref.dtype)
    joined_ref[0:rows] = jnp.where(high == 0, mine, other)
    joined_ref[rows:] = jnp.where(high == 0, other, mine)


def total_and_join_kernel(bit, pieces_ref, mine_ref, other_ref, out_ref, joined_ref):
    total = total_of(pieces_ref, 0, SLICE).astype(out_ref.dtype)
    for j in range(out_ref.shape[0]):
        out_ref[j] = total
    join(bit, mine_ref, other_ref, joined_ref)


def total_and_join(bit, pieces, mine, other, copies, kind):
    return pl.pallas_call(
        functools.partial(total_and_join_kernel, bit),
        out_shape=(
            jax.ShapeDtypeStruct((copies, SLICE, CLEN), kind),
            jax.ShapeDtypeStruct((2 * mine.shape[0], CLEN), BF),
        ),
        in_specs=[VM, VM, VM],
        out_specs=(VM, VM),
        compiler_params=SMALL,
        cost_estimate=pl.CostEstimate(flops=90000, bytes_accessed=500000, transcendentals=0),
    )(pieces, mine, other)


def finish_kernel(pieces_ref, mine_ref, other_ref, prompt_ref, comp_ref, joined_ref):
    join(2, mine_ref, other_ref, joined_ref)
    comp_ref[...] = joined_ref[0:DQK].astype(F32)
    for core in range(2):
        for j in range(HALF // SLICE):
            first = HALF * core + SLICE * j
            prompt_ref[first : first + SLICE] = pieces_ref[2 * j + core].astype(F32)


def finish(pieces, mine, other):
    return pl.pallas_call(
        finish_kernel,
        out_shape=(jax.ShapeDtypeStruct((DQK, CLEN), F32), jax.ShapeDtypeStruct((DQK, CLEN), F32)),
        in_specs=[VM, VM, VM],
        out_specs=(VM, VM),
        scratch_shapes=[pltpu.VMEM((WIDE, CLEN), BF)],
        compiler_params=SMALL,
        cost_estimate=pl.CostEstimate(flops=90000, bytes_accessed=900000, transcendentals=0),
    )(pieces, mine, other)


def swap(block, axis, count, bit):
    return lax.ppermute(block, axis, [(i, i ^ bit) for i in range(count)])


def on_device(queries, grad_out, prompt_kv, comp_kv, lengths):
    half = lax.dynamic_slice(prompt_kv, (HALF * lax.axis_index("c"), 0), (HALF, CLEN))
    mine = lax.all_to_all(jnp.broadcast_to(half[None], (8, HALF, CLEN)), HS, 0, 0)
    left = turn(queries, grad_out)
    mine = after(mine, left)
    other = swap(mine, "c", 2, 1)
    send, keep, tall = main(lengths, queries, grad_out, left, mine, other, comp_kv)
    terms = lax.all_to_all(cores_sum(keep, swap(send, "c", 2, 1)), HS, 0, 0)
    grad_queries, tall = query_grads(tall)
    prompt_part, comp = heads_sum(terms, tall)
    pieces = lax.all_to_all(prompt_part.reshape(8, SLICE, CLEN), "z", 0, 0)
    pieces, comp = total_and_join(0, pieces, comp, swap(comp, "x", 4, 1), 4, F32)
    pieces = lax.all_to_all(pieces, "yh", 0, 0)
    pieces, comp = total_and_join(1, pieces, comp, swap(comp, "x", 4, 2), 16, BF)
    pieces = lax.all_to_all(pieces, ("z", "c"), 0, 0)
    grad_prompt, grad_comp = finish(pieces, comp, swap(comp, "yl", 2, 1))
    return (grad_queries, grad_prompt, grad_comp)


def solution(mesh):
    parts = Mesh(mesh.devices.reshape(4, 8, 2, 2, 4), CTX + HS)
    in_specs = (P(CTX, HS), P(CTX, HS), P(None, HS), P(None, CTX), P())
    out_specs = (P(CTX, HS), P(None, HS), P(None, CTX))
    return jax.shard_map(
        on_device, mesh=parts, in_specs=in_specs, out_specs=out_specs, check_vma=False
    )
```

time: 112 us -> 104 us (0.929)
  Pallas kernels: 23.9 us -> 18 us
  waiting for transfers between devices: 36.6 us -> 31.1 us
  starting transfers between devices: 45.5 us -> 49.4 us
    ppermute x3 -> x5, starting transfers between devices: 8.05 us -> 18 us  [swap(): return lax.ppermute(block, axis, [(i, i ^ bit) for i in range(count)])]
    all_to_all x5, waiting for transfers between devices: 28.2 us -> 19.2 us  [the longest x1 6.56 us: on_device(): terms = lax.all_to_all(cores_sum(keep, swap(send, 'c', 2, 1)), HS, 0, 0)]
    all_to_all x5, starting transfers between devices: 37.5 us -> 31.4 us  [the longest x1 8.09 us: on_device(): pieces = lax.all_to_all(pieces, ('z', 'c'), 0, 0)]
    ppermute x3 -> x5, waiting for transfers between devices: 8.32 us -> 11.9 us  [swap(): return lax.ppermute(block, axis, [(i, i ^ bit) for i in range(count)])]
    pallas_call x1, Pallas kernels: 3.76 us -> 0.73 us  [turn(): pl.pallas_call(turn_kernel, out_shape=jax.ShapeDtypeStruct((DQK, 2 * ROWS...]
    pallas_call x4 -> x6, Pallas kernels: 13.9 us -> 11.3 us  [the longest x1 8.21 us: main(): pl.pallas_call(main_kernel, out_shape=(jax.ShapeDtypeStruct((8, HALF, CLE...]
    unnamed x6 -> x14, local copies, waits for them, and re-layouts: 1.74 us -> 3.42 us
    broadcast_in_dim x1, local copies, waits for them, and re-layouts: 2.08 us -> 0.89 us  [on_device(): jnp.broadcast_to(half[None], (8, HALF, CLEN))]
  transfers between devices with their start and end apart: 8 -> 10, of which waited for: 8 -> 10; matrix products, arithmetic and copies ran while one was open for 1% -> 0% of each run, Pallas kernels for 8% -> 6%
where the time goes in v3:
time: 104 us
  starting transfers between devices  49.4 us (48%)
  waiting for transfers between devices  31.1 us (30%)
  Pallas kernels  18 us (17%)
  local copies, waits for them, and re-layouts  4.31 us (4%)
    ppermute x5, starting transfers between devices, swap(): return lax.ppermute(block, axis, [(i, i ^ bit) for i in range(count)])  18 us
    ppermute x5, waiting for transfers between devices, swap(): return lax.ppermute(block, axis, [(i, i ^ bit) for i in range(count)])  11.9 us
    pallas_call x1, Pallas kernels, main(): pl.pallas_call(main_kernel, out_shape=(jax.ShapeDtypeStruct((8, HALF, CLE...  8.21 us
    all_to_all x1, starting transfers between devices, on_device(): pieces = lax.all_to_all(pieces, ('z', 'c'), 0, 0)  8.09 us
    all_to_all x1, starting transfers between devices, on_device(): pieces = lax.all_to_all(prompt_part.reshape(8, SLICE, CLEN), 'z', 0, 0)  7.99 us
    all_to_all x1, waiting for transfers between devices, on_device(): terms = lax.all_to_all(cores_sum(keep, swap(send, 'c', 2, 1)), HS, 0, 0)  6.56 us
    all_to_all x1, starting transfers between devices, on_device(): pieces = lax.all_to_all(pieces, 'yh', 0, 0)  5.92 us
    all_to_all x1, starting transfers between devices, on_device(): lax.all_to_all(jnp.broadcast_to(half[None], (8, HALF, CLEN)), HS, 0, 0)  5.86 us
  transfers between devices with their start and end apart: 10, of which 10 were waited for; matrix products, arithmetic and copies ran while one was open for 0% of the time, Pallas kernels for 6%

profile of v3, /device:TPU:1, one launch (start us, length us, event | category | flops | bytes accessed | tf_op | source)
XLA Modules:
  0.0 103.6 jit_solution(3694185402664583709)
XLA Ops:
  0.6 0.0 copy-start
  0.6 0.9 copy-done
  1.6 0.9 broadcast_in_dim.2
  2.4 5.9 %all-to-all-start = ((bf16[8,288,128]{2,1,0:T(8,128)(2,1)}), bf16[8,288,128]{2,1,0:T(8,128)(2,1)S(1)}, u32[]{:S(2)}, u32[]{:S(2)}) async-start(bf16[8,288,128]{2,1,0:T(8,128)(2,1)} %broadcast_in_dim.2), calls=%async_computation | async-start | bytes 1179648 | tf_op jit(solution)/shard_map/all_to_all | solution.py:318
  8.3 0.0 copy-start.1
  8.3 1.3 %copy-done.1 = bf16[128,4608]{1,0:T(8,128)(2,1)S(1)} copy-done((bf16[128,4608]{1,0:T(8,128)(2,1)S(1)}, bf16[128,4608]{1,0:T(8,128)(2,1)}, u32[]{:S(2)}) %copy-start.1) | copy-done | bytes 1179672
  9.6 0.0 copy-start.3
  9.6 1.2 %copy-done.3 = bf16[128,4096]{1,0:T(8,128)(2,1)S(1)} copy-done((bf16[128,4096]{1,0:T(8,128)(2,1)S(1)}, bf16[128,4096]{1,0:T(8,128)(2,1)}, u32[]{:S(2)}) %copy-start.3) | copy-done | bytes 1048600
  10.8 0.7 shard_map.76.done_ref.left_ref
  11.5 0.0 copy-start.5
  11.6 0.0 copy-start.6
  11.6 4.1 %all-to-all-done.block_ref = bf16[8,288,128]{2,1,0:T(8,128)(2,1)S(1)} async-done(((bf16[8,288,128]{2,1,0:T(8,128)(2,1)}), bf16[8,288,128]{2,1,0:T(8,128)(2,1)S(1)}, u32[]{:S(2)}, u32[]{:S(2)}) %all-to-all-start) | async-done | bytes 589856 | tf_op jit(solution)/shard_map/all_to_all | solution.py:318
  15.7 0.0 copy-start.2
  15.7 0.0 copy-start.4
  15.7 7.7 %collective-permute-start = (bf16[8,288,128]{2,1,0:T(8,128)(2,1)S(1)}, bf16[8,288,128]{2,1,0:T(8,128)(2,1)S(1)}, u32[]{:S(2)}, u32[]{:S(2)}) collective-permute-start(bf16[8,288,128]{2,1,0:T(8,128)(2,1)S(1)} %shard_map.77.mine_ref), channel_id=1, source_target_pairs={{0,8},{8,0},{1,9},{9,1},{2,10},{10,2},{3,11},{11,3},{4,12},{12,4},... | collective-permute-start | bytes 1769480 | tf_op jit(solution)/shard_map/ppermute | solution.py:313
  23.4 1.6 %collective-permute-done.other_ref = bf16[8,288,128]{2,1,0:T(8,128)(2,1)S(1)} collective-permute-done((bf16[8,288,128]{2,1,0:T(8,128)(2,1)S(1)}, bf16[8,288,128]{2,1,0:T(8,128)(2,1)S(1)}, u32[]{:S(2)}, u32[]{:S(2)}) %collective-permute-start) | collective-permute-done | bytes 589856 | tf_op jit(solution)/shard_map/ppermute | solution.py:313
  25.0 0.0 copy-done.5
  25.0 0.0 copy-done.6
  25.0 0.0 copy-done.2
  25.0 0.0 copy-done.4
  25.0 8.2 %shard_map.78 = (bf16[8,288,128]{2,1,0:T(8,128)(2,1)S(1)}, bf16[8,368,128]{2,1,0:T(8,128)(2,1)S(1)}, bf16[9216,1152]{1,0:T(8,128)(2,1)}) custom-call(s32[64]{0:T(128)S(1)} %copy-done.6, bf16[128,4608]{1,0:T(8,128)(2,1)S(1)} %copy-done.2, bf16[128,4096]{1,0:T(8,128)(2,1)S(1)} %copy-done.4, bf16[576,2048]{1,0:T(8,128)(2,1)S(1)} %shard_map.76.done_ref.left_ref, ...), custom_call_target="tpu_custom_call" | custom-call | flops 5200000000 | bytes 12000000 | tf_op jit(solution)/shard_map/pallas_call | solution.py:152
  33.2 2.3 %collective-permute-start.1 = (bf16[8,288,128]{2,1,0:T(8,128)(2,1)S(1)}, bf16[8,288,128]{2,1,0:T(8,128)(2,1)S(1)}, u32[]{:S(2)}, u32[]{:S(2)}) collective-permute-start(bf16[8,288,128]{2,1,0:T(8,128)(2,1)S(1)} %get-tuple-element.19), channel_id=1, source_target_pairs={{0,8},{8,0},{1,9},{9,1},{2,10},{10,2},{3,11},{11,3},{4,12},{12,4},... | collective-permute-start | bytes 1769480 | tf_op jit(solution)/shard_map/ppermute | solution.py:313
  35.5 1.6 %collective-permute-done.1.got_ref = bf16[8,288,128]{2,1,0:T(8,128)(2,1)S(1)} collective-permute-done((bf16[8,288,128]{2,1,0:T(8,128)(2,1)S(1)}, bf16[8,288,128]{2,1,0:T(8,128)(2,1)S(1)}, u32[]{:S(2)}, u32[]{:S(2)}) %collective-permute-start.1) | collective-permute-done | bytes 589856 | tf_op jit(solution)/shard_map/ppermute | solution.py:313
  37.1 1.0 %shard_map.80 = bf16[8,368,128]{2,1,0:T(8,128)(2,1)} custom-call(bf16[8,368,128]{2,1,0:T(8,128)(2,1)S(1)} %get-tuple-element.18.keep_ref, bf16[8,288,128]{2,1,0:T(8,128)(2,1)S(1)} %collective-permute-done.1.got_ref), custom_call_target="tpu_custom_call" | custom-call | flops 300000 | bytes 2100000 | tf_op jit(solution)/shard_map/pallas_call | solution.py:226
  38.2 3.5 %all-to-all-start.1 = ((bf16[8,368,128]{2,1,0:T(8,128)(2,1)}), bf16[8,368,128]{2,1,0:T(8,128)(2,1)S(1)}, u32[]{:S(2)}, u32[]{:S(2)}) async-start(bf16[8,368,128]{2,1,0:T(8,128)(2,1)} %shard_map.80), calls=%async_computation.1 | async-start | bytes 1507328 | tf_op jit(solution)/shard_map/all_to_all | solution.py:323
  41.7 5.1 %shard_map.79 = (bf16[128,4608]{1,0:T(8,128)(2,1)}, bf16[9216,1152]{1,0:T(8,128)(2,1)}) custom-call(bf16[9216,1152]{1,0:T(8,128)(2,1)} %get-tuple-element.16.tall_hbm), custom_call_target="tpu_custom_call", output_to_operand_aliasing={{1}: (0, {})} | custom-call | flops 1400000000 | bytes 5000000 | tf_op jit(solution)/shard_map/pallas_call | solution.py:201
  46.8 6.6 %all-to-all-done.1.terms_ref = bf16[8,368,128]{2,1,0:T(8,128)(2,1)S(1)} async-done(((bf16[8,368,128]{2,1,0:T(8,128)(2,1)}), bf16[8,368,128]{2,1,0:T(8,128)(2,1)S(1)}, u32[]{:S(2)}, u32[]{:S(2)}) %all-to-all-start.1) | async-done | bytes 753696 | tf_op jit(solution)/shard_map/all_to_all | solution.py:323
  53.3 0.7 shard_map.81
  54.1 8.0 %all-to-all-start.2 = ((bf16[8,48,128]{2,1,0:T(8,128)(2,1)}), bf16[8,48,128]{2,1,0:T(8,128)(2,1)S(1)}, u32[]{:S(2)}, u32[]{:S(2)}) async-start(bf16[8,48,128]{2,1,0:T(8,128)(2,1)} %bitcast), calls=%async_computation.2 | async-start | bytes 196608 | tf_op jit(solution)/shard_map/all_to_all | solution.py:326
  62.1 2.1 %collective-permute-start.2 = (bf16[80,128]{1,0:T(8,128)(2,1)S(1)}, bf16[80,128]{1,0:T(8,128)(2,1)S(1)}, u32[]{:S(2)}, u32[]{:S(2)}) collective-permute-start(bf16[80,128]{1,0:T(8,128)(2,1)S(1)} %get-tuple-element.22.mine_ref), channel_id=1, source_target_pairs={{0,1},{1,0},{2,3},{3,2},{4,5},{5,4},{6,7},{7,6},{8,9},{9,8},{10,11... | collective-permute-start | bytes 61448 | tf_op jit(solution)/shard_map/ppermute | solution.py:313
  64.2 2.5 %collective-permute-done.2.other_ref = bf16[80,128]{1,0:T(8,128)(2,1)S(1)} collective-permute-done((bf16[80,128]{1,0:T(8,128)(2,1)S(1)}, bf16[80,128]{1,0:T(8,128)(2,1)S(1)}, u32[]{:S(2)}, u32[]{:S(2)}) %collective-permute-start.2) | collective-permute-done | bytes 20512 | tf_op jit(solution)/shard_map/ppermute | solution.py:313
  66.7 3.0 %all-to-all-done.2.pieces_ref = bf16[8,48,128]{2,1,0:T(8,128)(2,1)S(1)} async-done(((bf16[8,48,128]{2,1,0:T(8,128)(2,1)}), bf16[8,48,128]{2,1,0:T(8,128)(2,1)S(1)}, u32[]{:S(2)}, u32[]{:S(2)}) %all-to-all-start.2) | async-done | bytes 98336 | tf_op jit(solution)/shard_map/all_to_all | solution.py:326
  69.7 0.7 shard_map.82
  70.4 5.9 %all-to-all-start.3 = ((f32[4,48,128]{2,1,0:T(8,128)}), f32[4,48,128]{2,1,0:T(8,128)S(1)}, u32[]{:S(2)}, u32[]{:S(2)}) async-start(f32[4,48,128]{2,1,0:T(8,128)} %get-tuple-element.23), calls=%async_computation.3 | async-start | bytes 196608 | tf_op jit(solution)/shard_map/all_to_all | solution.py:328
  76.3 3.1 %collective-permute-start.3 = (bf16[160,128]{1,0:T(8,128)(2,1)S(1)}, bf16[160,128]{1,0:T(8,128)(2,1)S(1)}, u32[]{:S(2)}, u32[]{:S(2)}) collective-permute-start(bf16[160,128]{1,0:T(8,128)(2,1)S(1)} %get-tuple-element.24.mine_ref), channel_id=1, source_target_pairs={{0,2},{1,3},{2,0},{3,1},{4,6},{5,7},{6,4},{7,5},{8,10},{9,11},{10,... | collective-permute-start | bytes 122888 | tf_op jit(solution)/shard_map/ppermute | solution.py:313
  79.4 3.2 %collective-permute-done.3.other_ref = bf16[160,128]{1,0:T(8,128)(2,1)S(1)} collective-permute-done((bf16[160,128]{1,0:T(8,128)(2,1)S(1)}, bf16[160,128]{1,0:T(8,128)(2,1)S(1)}, u32[]{:S(2)}, u32[]{:S(2)}) %collective-permute-start.3) | collective-permute-done | bytes 40992 | tf_op jit(solution)/shard_map/ppermute | solution.py:313
  82.6 1.1 %all-to-all-done.3.pieces_ref = f32[4,48,128]{2,1,0:T(8,128)S(1)} async-done(((f32[4,48,128]{2,1,0:T(8,128)}), f32[4,48,128]{2,1,0:T(8,128)S(1)}, u32[]{:S(2)}, u32[]{:S(2)}) %all-to-all-start.3) | async-done | bytes 98336 | tf_op jit(solution)/shard_map/all_to_all | solution.py:328
  83.6 0.7 shard_map.83
  84.3 8.1 %all-to-all-start.4 = ((bf16[16,48,128]{2,1,0:T(8,128)(2,1)}), bf16[16,48,128]{2,1,0:T(8,128)(2,1)S(1)}, u32[]{:S(2)}, u32[]{:S(2)}) async-start(bf16[16,48,128]{2,1,0:T(8,128)(2,1)} %get-tuple-element.25), calls=%async_computation.4 | async-start | bytes 393216 | tf_op jit(solution)/shard_map/all_to_all | solution.py:330
  92.4 2.9 %collective-permute-start.4 = (bf16[320,128]{1,0:T(8,128)(2,1)S(1)}, bf16[320,128]{1,0:T(8,128)(2,1)S(1)}, u32[]{:S(2)}, u32[]{:S(2)}) collective-permute-start(bf16[320,128]{1,0:T(8,128)(2,1)S(1)} %get-tuple-element.26.mine_ref), channel_id=1, source_target_pairs={{0,4},{4,0},{1,5},{5,1},{2,6},{6,2},{3,7},{7,3},{8,12},{12,8},{9,1... | collective-permute-start | bytes 245768 | tf_op jit(solution)/shard_map/ppermute | solution.py:313
  95.3 3.0 %collective-permute-done.4.other_ref = bf16[320,128]{1,0:T(8,128)(2,1)S(1)} collective-permute-done((bf16[320,128]{1,0:T(8,128)(2,1)S(1)}, bf16[320,128]{1,0:T(8,128)(2,1)S(1)}, u32[]{:S(2)}, u32[]{:S(2)}) %collective-permute-start.4) | collective-permute-done | bytes 81952 | tf_op jit(solution)/shard_map/ppermute | solution.py:313
  98.3 4.4 %all-to-all-done.4.pieces_ref = bf16[16,48,128]{2,1,0:T(8,128)(2,1)S(1)} async-done(((bf16[16,48,128]{2,1,0:T(8,128)(2,1)}), bf16[16,48,128]{2,1,0:T(8,128)(2,1)S(1)}, u32[]{:S(2)}, u32[]{:S(2)}) %all-to-all-start.4) | async-done | bytes 196640 | tf_op jit(solution)/shard_map/all_to_all | solution.py:330
  102.7 0.9 shard_map.84
  (2 shorter events, 0.0 us)
Async XLA Ops:
  0.6 0.9 copy-start
  2.4 13.3 %all-to-all-start = ((bf16[8,288,128]{2,1,0:T(8,128)(2,1)}), bf16[8,288,128]{2,1,0:T(8,128)(2,1)S(1)}, u32[]{:S(2)}, u32[]{:S(2)}) async-start(bf16[8,288,128]{2,1,0:T(8,128)(2,1)} %broadcast_in_dim.2), calls=%async_computation | async-start | bytes 1179648 | tf_op jit(solution)/shard_map/all_to_all | solution.py:318
  8.3 1.3 %copy-start.1 = (bf16[128,4608]{1,0:T(8,128)(2,1)S(1)}, bf16[128,4608]{1,0:T(8,128)(2,1)}, u32[]{:S(2)}) copy-start(bf16[128,4608]{1,0:T(8,128)(2,1)} %q_ref.3) | copy-start | bytes 3538948
  9.6 1.2 %copy-start.3 = (bf16[128,4096]{1,0:T(8,128)(2,1)S(1)}, bf16[128,4096]{1,0:T(8,128)(2,1)}, u32[]{:S(2)}) copy-start(bf16[128,4096]{1,0:T(8,128)(2,1)} %g_ref.3) | copy-start | bytes 3145732
  11.5 13.4 %copy-start.5 = (bf16[576,128]{1,0:T(8,128)(2,1)S(1)}, bf16[576,128]{1,0:T(8,128)(2,1)}, u32[]{:S(2)}) copy-start(bf16[576,128]{1,0:T(8,128)(2,1)} %comp_ref.1) | copy-start | bytes 442372
  11.6 13.4 %copy-start.6 = (s32[64]{0:T(128)S(1)}, s32[64]{0:T(128)}, u32[]{:S(2)}) copy-start(s32[64]{0:T(128)} %lengths_ref.1) | copy-start | bytes 772
  15.7 9.3 %copy-start.2 = (bf16[128,4608]{1,0:T(8,128)(2,1)S(1)}, bf16[128,4608]{1,0:T(8,128)(2,1)}, u32[]{:S(2)}) copy-start(bf16[128,4608]{1,0:T(8,128)(2,1)} %q_ref.3) | copy-start | bytes 3538948
  15.7 9.3 %copy-start.4 = (bf16[128,4096]{1,0:T(8,128)(2,1)S(1)}, bf16[128,4096]{1,0:T(8,128)(2,1)}, u32[]{:S(2)}) copy-start(bf16[128,4096]{1,0:T(8,128)(2,1)} %g_ref.3) | copy-start | bytes 3145732
  15.7 9.3 %collective-permute-start = (bf16[8,288,128]{2,1,0:T(8,128)(2,1)S(1)}, bf16[8,288,128]{2,1,0:T(8,128)(2,1)S(1)}, u32[]{:S(2)}, u32[]{:S(2)}) collective-permute-start(bf16[8,288,128]{2,1,0:T(8,128)(2,1)S(1)} %shard_map.77.mine_ref), channel_id=1, source_target_pairs={{0,8},{8,0},{1,9},{9,1},{2,10},{10,2},{3,11},{11,3},{4,12},{12,4},... | collective-permute-start | bytes 1769480 | tf_op jit(solution)/shard_map/ppermute | solution.py:313
  33.2 3.9 %collective-permute-start.1 = (bf16[8,288,128]{2,1,0:T(8,128)(2,1)S(1)}, bf16[8,288,128]{2,1,0:T(8,128)(2,1)S(1)}, u32[]{:S(2)}, u32[]{:S(2)}) collective-permute-start(bf16[8,288,128]{2,1,0:T(8,128)(2,1)S(1)} %get-tuple-element.19), channel_id=1, source_target_pairs={{0,8},{8,0},{1,9},{9,1},{2,10},{10,2},{3,11},{11,3},{4,12},{12,4},... | collective-permute-start | bytes 1769480 | tf_op jit(solution)/shard_map/ppermute | solution.py:313
  38.2 15.2 %all-to-all-start.1 = ((bf16[8,368,128]{2,1,0:T(8,128)(2,1)}), bf16[8,368,128]{2,1,0:T(8,128)(2,1)S(1)}, u32[]{:S(2)}, u32[]{:S(2)}) async-start(bf16[8,368,128]{2,1,0:T(8,128)(2,1)} %shard_map.80), calls=%async_computation.1 | async-start | bytes 1507328 | tf_op jit(solution)/shard_map/all_to_all | solution.py:323
  54.1 15.7 %all-to-all-start.2 = ((bf16[8,48,128]{2,1,0:T(8,128)(2,1)}), bf16[8,48,128]{2,1,0:T(8,128)(2,1)S(1)}, u32[]{:S(2)}, u32[]{:S(2)}) async-start(bf16[8,48,128]{2,1,0:T(8,128)(2,1)} %bitcast), calls=%async_computation.2 | async-start | bytes 196608 | tf_op jit(solution)/shard_map/all_to_all | solution.py:326
  62.1 4.7 %collective-permute-start.2 = (bf16[80,128]{1,0:T(8,128)(2,1)S(1)}, bf16[80,128]{1,0:T(8,128)(2,1)S(1)}, u32[]{:S(2)}, u32[]{:S(2)}) collective-permute-start(bf16[80,128]{1,0:T(8,128)(2,1)S(1)} %get-tuple-element.22.mine_ref), channel_id=1, source_target_pairs={{0,1},{1,0},{2,3},{3,2},{4,5},{5,4},{6,7},{7,6},{8,9},{9,8},{10,11... | collective-permute-start | bytes 61448 | tf_op jit(solution)/shard_map/ppermute | solution.py:313
  70.4 13.2 %all-to-all-start.3 = ((f32[4,48,128]{2,1,0:T(8,128)}), f32[4,48,128]{2,1,0:T(8,128)S(1)}, u32[]{:S(2)}, u32[]{:S(2)}) async-start(f32[4,48,128]{2,1,0:T(8,128)} %get-tuple-element.23), calls=%async_computation.3 | async-start | bytes 196608 | tf_op jit(solution)/shard_map/all_to_all | solution.py:328
  76.3 6.2 %collective-permute-start.3 = (bf16[160,128]{1,0:T(8,128)(2,1)S(1)}, bf16[160,128]{1,0:T(8,128)(2,1)S(1)}, u32[]{:S(2)}, u32[]{:S(2)}) collective-permute-start(bf16[160,128]{1,0:T(8,128)(2,1)S(1)} %get-tuple-element.24.mine_ref), channel_id=1, source_target_pairs={{0,2},{1,3},{2,0},{3,1},{4,6},{5,7},{6,4},{7,5},{8,10},{9,11},{10,... | collective-permute-start | bytes 122888 | tf_op jit(solution)/shard_map/ppermute | solution.py:313
  84.3 18.4 %all-to-all-start.4 = ((bf16[16,48,128]{2,1,0:T(8,128)(2,1)}), bf16[16,48,128]{2,1,0:T(8,128)(2,1)S(1)}, u32[]{:S(2)}, u32[]{:S(2)}) async-start(bf16[16,48,128]{2,1,0:T(8,128)(2,1)} %get-tuple-element.25), calls=%async_computation.4 | async-start | bytes 393216 | tf_op jit(solution)/shard_map/all_to_all | solution.py:330
  92.4 5.9 %collective-permute-start.4 = (bf16[320,128]{1,0:T(8,128)(2,1)S(1)}, bf16[320,128]{1,0:T(8,128)(2,1)S(1)}, u32[]{:S(2)}, u32[]{:S(2)}) collective-permute-start(bf16[320,128]{1,0:T(8,128)(2,1)S(1)} %get-tuple-element.26.mine_ref), channel_id=1, source_target_pairs={{0,4},{4,0},{1,5},{5,1},{2,6},{6,2},{3,7},{7,3},{8,12},{12,8},{9,1... | collective-permute-start | bytes 245768 | tf_op jit(solution)/shard_map/ppermute | solution.py:313

commit v4 on v3

--- a/solution.py
+++ b/solution.py
@@ -41,7 +41,9 @@
     return lax.dot_general(a, b, ((contract[0:1], contract[1:2]), ((), ())), preferred_element_type=F32)
 
 
-def turn_kernel(q_ref, g_ref, left_ref):
+def turn_kernel(lengths_ref, q_ref, g_ref, left_ref, alive_ref):
+    slot = lax.broadcasted_iota(jnp.int32, (CLEN, CLEN), 0)
+    alive_ref[...] = (slot < lengths_ref[lax.axis_index(CTX)]).astype(F32)
     for i, h in enumerate(ORDER):
         part = q_ref[:, 1152 * (h // 2) + 512 * (h % 2) : 1152 * (h // 2) + 512 * (h % 2) + WIDE]
         turned = part.T
@@ -51,15 +53,15 @@
     left_ref[D_LAT:DQK, ROWS:] = jnp.zeros((DQK - D_LAT, ROWS), BF)
 
 
-def turn(queries, grad_out):
+def turn(lengths, queries, grad_out):
     return pl.pallas_call(
         turn_kernel,
-        out_shape=jax.ShapeDtypeStruct((DQK, 2 * ROWS), BF),
-        in_specs=[VM, VM],
-        out_specs=VM,
+        out_shape=(jax.ShapeDtypeStruct((DQK, 2 * ROWS), BF), jax.ShapeDtypeStruct((CLEN, CLEN), F32)),
+        in_specs=[pl.BlockSpec(memory_space=pltpu.SMEM), VM, VM],
+        out_specs=(VM, VM),
         compiler_params=PARAMS,
         cost_estimate=pl.CostEstimate(flops=0, bytes_accessed=4600000, transcendentals=0),
-    )(queries, grad_out)
+    )(lengths, queries, grad_out)
 
 
 def after_kernel(block_ref, done_ref, out_ref):
@@ -78,8 +80,8 @@
     )(block, done)
 
 
-def main_kernel(lengths_ref, q_ref, g_ref, left_ref, mine_ref, other_ref, comp_ref, send_ref, keep_ref, tall_hbm, right_ref, keys_ref, score_ref, gprob_ref, sems):
-    live, core = lengths_ref[lax.axis_index(CTX)], lax.axis_index("c")
+def main_kernel(alive_ref, q_ref, g_ref, left_ref, mine_ref, other_ref, comp_ref, send_ref, keep_ref, tall_hbm, right_ref, keys_ref, score_ref, gprob_ref, sems):
+    core = lax.axis_index("c")
     zero = jnp.zeros((EDGE, KEYS), BF)
     keys_ref[0:EDGE] = zero
     keys_ref[EDGE + DQK :] = zero
@@ -109,7 +111,7 @@
             largest = jnp.max(score, axis=1, keepdims=True)
             weight = jnp.exp2((score - largest) * (score_scale * LOG2E))
             total = jnp.sum(weight, axis=1, keepdims=True)
-            alive = (slot[:, :1] < live).astype(F32)
+            alive = alive_ref[r % CLEN : r % CLEN + 16, :1]
             prob = weight * (alive / total)
             gprob = gprob_ref[r : r + 16]
             delta = jnp.sum(prob * gprob, axis=1, keepdims=True)
@@ -148,7 +150,7 @@
         move.wait()
 
 
-def main(lengths, queries, grad_out, left, mine, other, comp):
+def main(alive, queries, grad_out, left, mine, other, comp):
     return pl.pallas_call(
         main_kernel,
         out_shape=(
@@ -156,7 +158,7 @@
             jax.ShapeDtypeStruct((8, HALF + PIECE, CLEN), BF),
             jax.ShapeDtypeStruct((TALL, KEYS), BF),
         ),
-        in_specs=[pl.BlockSpec(memory_space=pltpu.SMEM)] + [VM] * 6,
+        in_specs=[VM] * 7,
         out_specs=(VM, VM, HBM),
         scratch_shapes=[
             pltpu.VMEM((2 * ROWS, KEYS), BF),
@@ -167,7 +169,7 @@
         ],
         compiler_params=PARAMS,
         cost_estimate=pl.CostEstimate(flops=5200000000, bytes_accessed=12000000, transcendentals=1200000),
-    )(lengths, queries, grad_out, left, mine, other, comp)
+    )(alive, queries, grad_out, left, mine, other, comp)
 
 
 def query_kernel(tall_hbm, out_hbm, same_hbm, grad_ref, keys_ref, out_ref, in_sems, out_sems):
@@ -244,13 +246,13 @@
     del tall_hbm
     prompt_ref[0:HALF] = total_of(terms_ref, 0, HALF).astype(BF)
     prompt_ref[HALF:] = jnp.zeros((8 * SLICE - HALF, CLEN), BF)
-    comp_ref[...] = total_of(terms_ref, HALF, PIECE).astype(BF)
+    comp_ref[0] = total_of(terms_ref, HALF, PIECE).astype(BF)
 
 
 def heads_sum(terms, tall):
     return pl.pallas_call(
         heads_sum_kernel,
-        out_shape=(jax.ShapeDtypeStruct((8 * SLICE, CLEN), BF), jax.ShapeDtypeStruct((PIECE, CLEN), BF)),
+        out_shape=(jax.ShapeDtypeStruct((8 * SLICE, CLEN), BF), jax.ShapeDtypeStruct((1, PIECE, CLEN), BF)),
         in_specs=[VM, HBM],
         out_specs=(VM, VM),
         compiler_params=PARAMS,
@@ -258,28 +260,28 @@
     )(terms, tall)
 
 
-def join(bit, mine_ref, other_ref, joined_ref):
-    axis, value = (("x", 1), ("x", 2), ("yl", 1))[bit]
-    high = lax.axis_index(axis) & value
-    rows = mine_ref.shape[0]
-    mine, other = mine_ref[...].astype(joined_ref.dtype), other_ref[...].astype(joined_ref.dtype)
-    joined_ref[0:rows] = jnp.where(high == 0, mine, other)
-    joined_ref[rows:] = jnp.where(high == 0, other, mine)
-
-
-def total_and_join_kernel(bit, pieces_ref, mine_ref, other_ref, out_ref, joined_ref):
+def spread_kernel(pieces_ref, out_ref):
     total = total_of(pieces_ref, 0, SLICE).astype(out_ref.dtype)
     for j in range(out_ref.shape[0]):
         out_ref[j] = total
-    join(bit, mine_ref, other_ref, joined_ref)
-
-
-def total_and_join(bit, pieces, mine, other, copies, kind):
-    return pl.pallas_call(
-        functools.partial(total_and_join_kernel, bit),
+
+
+def join_kernel(axis, pieces_ref, mine_ref, other_ref, out_ref, joined_ref):
+    spread_kernel(pieces_ref, out_ref)
+    even = (lax.axis_index(axis) & 1) == 0
+    count = mine_ref.shape[0]
+    for k in range(count):
+        mine, other = mine_ref[k].astype(F32), other_ref[k].astype(F32)
+        joined_ref[k] = jnp.where(even, mine, other).astype(BF)
+        joined_ref[count + k] = jnp.where(even, other, mine).astype(BF)
+
+
+def sum_and_join(axis, pieces, copies, kind, mine, other):
+    return pl.pallas_call(
+        functools.partial(join_kernel, axis),
         out_shape=(
             jax.ShapeDtypeStruct((copies, SLICE, CLEN), kind),
-            jax.ShapeDtypeStruct((2 * mine.shape[0], CLEN), BF),
+            jax.ShapeDtypeStruct((2 * mine.shape[0], PIECE, CLEN), BF),
         ),
         in_specs=[VM, VM, VM],
         out_specs=(VM, VM),
@@ -288,9 +290,16 @@
     )(pieces, mine, other)
 
 
-def finish_kernel(pieces_ref, mine_ref, other_ref, prompt_ref, comp_ref, joined_ref):
-    join(2, mine_ref, other_ref, joined_ref)
-    comp_ref[...] = joined_ref[0:DQK].astype(F32)
+def finish_kernel(pieces_ref, mine_ref, other_ref, prompt_ref, comp_ref):
+    low = (lax.axis_index("x") & 2) == 0
+    for odd in range(2):
+        for yl in range(2):
+            mine, other = mine_ref[2 * odd + yl].astype(F32), other_ref[2 * odd + yl].astype(F32)
+            for high in range(2):
+                first = PIECE * (4 * yl + 2 * high + odd)
+                rows = min(PIECE, DQK - first)
+                chunk = jnp.where(low, other, mine) if high else jnp.where(low, mine, other)
+                comp_ref[first : first + rows] = chunk[:rows]
     for core in range(2):
         for j in range(HALF // SLICE):
             first = HALF * core + SLICE * j
@@ -303,7 +312,6 @@
         out_shape=(jax.ShapeDtypeStruct((DQK, CLEN), F32), jax.ShapeDtypeStruct((DQK, CLEN), F32)),
         in_specs=[VM, VM, VM],
         out_specs=(VM, VM),
-        scratch_shapes=[pltpu.VMEM((WIDE, CLEN), BF)],
         compiler_params=SMALL,
         cost_estimate=pl.CostEstimate(flops=90000, bytes_accessed=900000, transcendentals=0),
     )(pieces, mine, other)
@@ -316,19 +324,19 @@
 def on_device(queries, grad_out, prompt_kv, comp_kv, lengths):
     half = lax.dynamic_slice(prompt_kv, (HALF * lax.axis_index("c"), 0), (HALF, CLEN))
     mine = lax.all_to_all(jnp.broadcast_to(half[None], (8, HALF, CLEN)), HS, 0, 0)
-    left = turn(queries, grad_out)
+    left, alive = turn(lengths, queries, grad_out)
     mine = after(mine, left)
     other = swap(mine, "c", 2, 1)
-    send, keep, tall = main(lengths, queries, grad_out, left, mine, other, comp_kv)
+    send, keep, tall = main(alive, queries, grad_out, left, mine, other, comp_kv)
     terms = lax.all_to_all(cores_sum(keep, swap(send, "c", 2, 1)), HS, 0, 0)
     grad_queries, tall = query_grads(tall)
     prompt_part, comp = heads_sum(terms, tall)
     pieces = lax.all_to_all(prompt_part.reshape(8, SLICE, CLEN), "z", 0, 0)
-    pieces, comp = total_and_join(0, pieces, comp, swap(comp, "x", 4, 1), 4, F32)
+    pieces, comp = sum_and_join("yl", pieces, 4, F32, comp, swap(comp, "yl", 2, 1))
     pieces = lax.all_to_all(pieces, "yh", 0, 0)
-    pieces, comp = total_and_join(1, pieces, comp, swap(comp, "x", 4, 2), 16, BF)
+    pieces, comp = sum_and_join("x", pieces, 16, BF, comp, swap(comp, "x", 4, 1))
     pieces = lax.all_to_all(pieces, ("z", "c"), 0, 0)
-    grad_prompt, grad_comp = finish(pieces, comp, swap(comp, "yl", 2, 1))
+    grad_prompt, grad_comp = finish(pieces, comp, swap(comp, "x", 4, 2))
     return (grad_queries, grad_prompt, grad_comp)
 
 

time: 104 us -> 104 us (level)
  waiting for transfers between devices: 31.1 us -> 29.7 us
    all_to_all x1, waiting for transfers between devices: 1.06 us -> 2.56 us  [on_device(): pieces = lax.all_to_all(pieces, 'yh', 0, 0)]
    all_to_all x1, waiting for transfers between devices: 4.43 us -> 2.92 us  [on_device(): pieces = lax.all_to_all(pieces, ('z', 'c'), 0, 0)]
    all_to_all x1, waiting for transfers between devices: 4.13 us -> 2.94 us  [on_device(): lax.all_to_all(jnp.broadcast_to(half[None], (8, HALF, CLEN)), HS, 0, 0)]
where the time goes in v4:
time: 104 us; the launch traced here: 103 us
  starting transfers between devices  49.6 us (48%)
  waiting for transfers between devices  29.7 us (29%)
  Pallas kernels  18.1 us (17%)
  local copies, waits for them, and re-layouts  4.96 us (5%)
    ppermute x5, starting transfers between devices, swap(): return lax.ppermute(block, axis, [(i, i ^ bit) for i in range(count)])  18.2 us
    ppermute x5, waiting for transfers between devices, swap(): return lax.ppermute(block, axis, [(i, i ^ bit) for i in range(count)])  11.7 us
    all_to_all x1, starting transfers between devices, on_device(): pieces = lax.all_to_all(pieces, ('z', 'c'), 0, 0)  8.09 us
    all_to_all x1, starting transfers between devices, on_device(): pieces = lax.all_to_all(prompt_part.reshape(8, SLICE, CLEN), 'z', 0, 0)  7.99 us
    pallas_call x1, Pallas kernels, main(): pl.pallas_call(main_kernel, out_shape=(jax.ShapeDtypeStruct((8, HALF, CLE...  7.76 us
    all_to_all x1, waiting for transfers between devices, on_device(): terms = lax.all_to_all(cores_sum(keep, swap(send, 'c', 2, 1)), HS, 0, 0)  6.56 us
    all_to_all x1, starting transfers between devices, on_device(): pieces = lax.all_to_all(pieces, 'yh', 0, 0)  5.91 us
    all_to_all x1, starting transfers between devices, on_device(): lax.all_to_all(jnp.broadcast_to(half[None], (8, HALF, CLEN)), HS, 0, 0)  5.86 us
  transfers between devices with their start and end apart: 10, of which 10 were waited for; matrix products, arithmetic and copies ran while one was open for 0% of the time, Pallas kernels for 6%

profile of v4, /device:TPU:1, one launch (start us, length us, event | category | flops | bytes accessed | tf_op | source)
XLA Modules:
  0.0 103.1 jit_solution(4587106744589032824)
XLA Ops:
  0.6 0.0 copy-start
  0.6 0.9 copy-done
  1.6 0.9 broadcast_in_dim.2
  2.4 5.9 %all-to-all-start = ((bf16[8,288,128]{2,1,0:T(8,128)(2,1)}), bf16[8,288,128]{2,1,0:T(8,128)(2,1)S(1)}, u32[]{:S(2)}, u32[]{:S(2)}) async-start(bf16[8,288,128]{2,1,0:T(8,128)(2,1)} %broadcast_in_dim.2), calls=%async_computation | async-start | bytes 1179648 | tf_op jit(solution)/shard_map/all_to_all | solution.py:326
  8.3 0.0 copy-start.1
  8.3 1.3 %copy-done.1 = bf16[128,4608]{1,0:T(8,128)(2,1)S(1)} copy-done((bf16[128,4608]{1,0:T(8,128)(2,1)S(1)}, bf16[128,4608]{1,0:T(8,128)(2,1)}, u32[]{:S(2)}) %copy-start.1) | copy-done | bytes 1179672
  9.6 0.0 copy-start.3
  9.6 1.2 %copy-done.3 = bf16[128,4096]{1,0:T(8,128)(2,1)S(1)} copy-done((bf16[128,4096]{1,0:T(8,128)(2,1)S(1)}, bf16[128,4096]{1,0:T(8,128)(2,1)}, u32[]{:S(2)}) %copy-start.3) | copy-done | bytes 1048600
  10.8 0.0 copy-start.5
  10.8 0.7 copy-done.5
  11.5 0.0 copy-start.6
  11.5 1.3 %shard_map.76 = (bf16[576,2048]{1,0:T(8,128)(2,1)S(1)}, f32[128,128]{1,0:T(8,128)S(1)}) custom-call(s32[64]{0:T(128)S(1)} %copy-done.5, bf16[128,4608]{1,0:T(8,128)(2,1)S(1)} %copy-done.1, bf16[128,4096]{1,0:T(8,128)(2,1)S(1)} %copy-done.3), custom_call_target="tpu_custom_call" | custom-call | bytes 4600000 | tf_op jit(solution)/shard_map/pallas_call | solution.py:57
  12.8 2.9 %all-to-all-done.block_ref = bf16[8,288,128]{2,1,0:T(8,128)(2,1)S(1)} async-done(((bf16[8,288,128]{2,1,0:T(8,128)(2,1)}), bf16[8,288,128]{2,1,0:T(8,128)(2,1)S(1)}, u32[]{:S(2)}, u32[]{:S(2)}) %all-to-all-start) | async-done | bytes 589856 | tf_op jit(solution)/shard_map/all_to_all | solution.py:326
  15.7 0.0 copy-start.2
  15.7 0.0 copy-start.4
  15.7 7.7 %collective-permute-start = (bf16[8,288,128]{2,1,0:T(8,128)(2,1)S(1)}, bf16[8,288,128]{2,1,0:T(8,128)(2,1)S(1)}, u32[]{:S(2)}, u32[]{:S(2)}) collective-permute-start(bf16[8,288,128]{2,1,0:T(8,128)(2,1)S(1)} %shard_map.77.mine_ref), channel_id=1, source_target_pairs={{0,8},{8,0},{1,9},{9,1},{2,10},{10,2},{3,11},{11,3},{4,12},{12,4},... | collective-permute-start | bytes 1769480 | tf_op jit(solution)/shard_map/ppermute | solution.py:321
  23.4 1.6 %collective-permute-done.other_ref = bf16[8,288,128]{2,1,0:T(8,128)(2,1)S(1)} collective-permute-done((bf16[8,288,128]{2,1,0:T(8,128)(2,1)S(1)}, bf16[8,288,128]{2,1,0:T(8,128)(2,1)S(1)}, u32[]{:S(2)}, u32[]{:S(2)}) %collective-permute-start) | collective-permute-done | bytes 589856 | tf_op jit(solution)/shard_map/ppermute | solution.py:321
  25.0 0.0 copy-done.6
  25.0 0.0 copy-done.2
  25.0 0.0 copy-done.4
  25.0 7.8 %shard_map.78 = (bf16[8,288,128]{2,1,0:T(8,128)(2,1)S(1)}, bf16[8,368,128]{2,1,0:T(8,128)(2,1)S(1)}, bf16[9216,1152]{1,0:T(8,128)(2,1)}) custom-call(f32[128,128]{1,0:T(8,128)S(1)} %get-tuple-element.18.alive_ref, bf16[128,4608]{1,0:T(8,128)(2,1)S(1)} %copy-done.2, bf16[128,4096]{1,0:T(8,128)(2,1)S(1)} %copy-done.4, ...), custom_call_target="tpu_custom_call" | custom-call | flops 5200000000 | bytes 12000000 | tf_op jit(solution)/shard_map/pallas_call | solution.py:154
  32.8 2.3 %collective-permute-start.1 = (bf16[8,288,128]{2,1,0:T(8,128)(2,1)S(1)}, bf16[8,288,128]{2,1,0:T(8,128)(2,1)S(1)}, u32[]{:S(2)}, u32[]{:S(2)}) collective-permute-start(bf16[8,288,128]{2,1,0:T(8,128)(2,1)S(1)} %get-tuple-element.23), channel_id=1, source_target_pairs={{0,8},{8,0},{1,9},{9,1},{2,10},{10,2},{3,11},{11,3},{4,12},{12,4},... | collective-permute-start | bytes 1769480 | tf_op jit(solution)/shard_map/ppermute | solution.py:321
  35.1 1.6 %collective-permute-done.1.got_ref = bf16[8,288,128]{2,1,0:T(8,128)(2,1)S(1)} collective-permute-done((bf16[8,288,128]{2,1,0:T(8,128)(2,1)S(1)}, bf16[8,288,128]{2,1,0:T(8,128)(2,1)S(1)}, u32[]{:S(2)}, u32[]{:S(2)}) %collective-permute-start.1) | collective-permute-done | bytes 589856 | tf_op jit(solution)/shard_map/ppermute | solution.py:321
  36.7 1.0 %shard_map.80 = bf16[8,368,128]{2,1,0:T(8,128)(2,1)} custom-call(bf16[8,368,128]{2,1,0:T(8,128)(2,1)S(1)} %get-tuple-element.22.keep_ref, bf16[8,288,128]{2,1,0:T(8,128)(2,1)S(1)} %collective-permute-done.1.got_ref), custom_call_target="tpu_custom_call" | custom-call | flops 300000 | bytes 2100000 | tf_op jit(solution)/shard_map/pallas_call | solution.py:228
  37.7 3.5 %all-to-all-start.1 = ((bf16[8,368,128]{2,1,0:T(8,128)(2,1)}), bf16[8,368,128]{2,1,0:T(8,128)(2,1)S(1)}, u32[]{:S(2)}, u32[]{:S(2)}) async-start(bf16[8,368,128]{2,1,0:T(8,128)(2,1)} %shard_map.80), calls=%async_computation.1 | async-start | bytes 1507328 | tf_op jit(solution)/shard_map/all_to_all | solution.py:331
  41.3 5.1 %shard_map.79 = (bf16[128,4608]{1,0:T(8,128)(2,1)}, bf16[9216,1152]{1,0:T(8,128)(2,1)}) custom-call(bf16[9216,1152]{1,0:T(8,128)(2,1)} %get-tuple-element.20.tall_hbm), custom_call_target="tpu_custom_call", output_to_operand_aliasing={{1}: (0, {})} | custom-call | flops 1400000000 | bytes 5000000 | tf_op jit(solution)/shard_map/pallas_call | solution.py:203
  46.3 6.6 %all-to-all-done.1.terms_ref = bf16[8,368,128]{2,1,0:T(8,128)(2,1)S(1)} async-done(((bf16[8,368,128]{2,1,0:T(8,128)(2,1)}), bf16[8,368,128]{2,1,0:T(8,128)(2,1)S(1)}, u32[]{:S(2)}, u32[]{:S(2)}) %all-to-all-start.1) | async-done | bytes 753696 | tf_op jit(solution)/shard_map/all_to_all | solution.py:331
  52.9 0.7 shard_map.81
  53.6 8.0 %all-to-all-start.2 = ((bf16[8,48,128]{2,1,0:T(8,128)(2,1)}), bf16[8,48,128]{2,1,0:T(8,128)(2,1)S(1)}, u32[]{:S(2)}, u32[]{:S(2)}) async-start(bf16[8,48,128]{2,1,0:T(8,128)(2,1)} %bitcast), calls=%async_computation.2 | async-start | bytes 196608 | tf_op jit(solution)/shard_map/all_to_all | solution.py:334
  61.6 3.2 %collective-permute-start.2 = (bf16[1,80,128]{2,1,0:T(8,128)(2,1)S(1)}, bf16[1,80,128]{2,1,0:T(8,128)(2,1)S(1)}, u32[]{:S(2)}, u32[]{:S(2)}) collective-permute-start(bf16[1,80,128]{2,1,0:T(8,128)(2,1)S(1)} %get-tuple-element.26.mine_ref), channel_id=1, source_target_pairs={{0,4},{4,0},{1,5},{5,1},{2,6},{6,2},{3,7},{7,3},{8,12},{12,8},{9,1... | collective-permute-start | bytes 61448 | tf_op jit(solution)/shard_map/ppermute | solution.py:321
  64.8 1.4 %collective-permute-done.2.other_ref = bf16[1,80,128]{2,1,0:T(8,128)(2,1)S(1)} collective-permute-done((bf16[1,80,128]{2,1,0:T(8,128)(2,1)S(1)}, bf16[1,80,128]{2,1,0:T(8,128)(2,1)S(1)}, u32[]{:S(2)}, u32[]{:S(2)}) %collective-permute-start.2) | collective-permute-done | bytes 20512 | tf_op jit(solution)/shard_map/ppermute | solution.py:321
  66.3 3.0 %all-to-all-done.2.pieces_ref = bf16[8,48,128]{2,1,0:T(8,128)(2,1)S(1)} async-done(((bf16[8,48,128]{2,1,0:T(8,128)(2,1)}), bf16[8,48,128]{2,1,0:T(8,128)(2,1)S(1)}, u32[]{:S(2)}, u32[]{:S(2)}) %all-to-all-start.2) | async-done | bytes 98336 | tf_op jit(solution)/shard_map/all_to_all | solution.py:334
  69.3 0.7 shard_map.82
  69.9 5.9 %all-to-all-start.3 = ((f32[4,48,128]{2,1,0:T(8,128)}), f32[4,48,128]{2,1,0:T(8,128)S(1)}, u32[]{:S(2)}, u32[]{:S(2)}) async-start(f32[4,48,128]{2,1,0:T(8,128)} %get-tuple-element.27), calls=%async_computation.3 | async-start | bytes 196608 | tf_op jit(solution)/shard_map/all_to_all | solution.py:336
  75.8 2.0 %collective-permute-start.3 = (bf16[2,80,128]{2,1,0:T(8,128)(2,1)S(1)}, bf16[2,80,128]{2,1,0:T(8,128)(2,1)S(1)}, u32[]{:S(2)}, u32[]{:S(2)}) collective-permute-start(bf16[2,80,128]{2,1,0:T(8,128)(2,1)S(1)} %get-tuple-element.28.mine_ref), channel_id=1, source_target_pairs={{0,1},{1,0},{2,3},{3,2},{4,5},{5,4},{6,7},{7,6},{8,9},{9,8},{10,11... | collective-permute-start | bytes 122888 | tf_op jit(solution)/shard_map/ppermute | solution.py:321
  77.9 2.7 %collective-permute-done.3.other_ref = bf16[2,80,128]{2,1,0:T(8,128)(2,1)S(1)} collective-permute-done((bf16[2,80,128]{2,1,0:T(8,128)(2,1)S(1)}, bf16[2,80,128]{2,1,0:T(8,128)(2,1)S(1)}, u32[]{:S(2)}, u32[]{:S(2)}) %collective-permute-start.3) | collective-permute-done | bytes 40992 | tf_op jit(solution)/shard_map/ppermute | solution.py:321
  80.6 2.6 %all-to-all-done.3.pieces_ref = f32[4,48,128]{2,1,0:T(8,128)S(1)} async-done(((f32[4,48,128]{2,1,0:T(8,128)}), f32[4,48,128]{2,1,0:T(8,128)S(1)}, u32[]{:S(2)}, u32[]{:S(2)}) %all-to-all-start.3) | async-done | bytes 98336 | tf_op jit(solution)/shard_map/all_to_all | solution.py:336
  83.1 0.7 shard_map.83
  83.8 8.1 %all-to-all-start.4 = ((bf16[16,48,128]{2,1,0:T(8,128)(2,1)}), bf16[16,48,128]{2,1,0:T(8,128)(2,1)S(1)}, u32[]{:S(2)}, u32[]{:S(2)}) async-start(bf16[16,48,128]{2,1,0:T(8,128)(2,1)} %get-tuple-element.29), calls=%async_computation.4 | async-start | bytes 393216 | tf_op jit(solution)/shard_map/all_to_all | solution.py:338
  91.9 3.0 %collective-permute-start.4 = (bf16[4,80,128]{2,1,0:T(8,128)(2,1)S(1)}, bf16[4,80,128]{2,1,0:T(8,128)(2,1)S(1)}, u32[]{:S(2)}, u32[]{:S(2)}) collective-permute-start(bf16[4,80,128]{2,1,0:T(8,128)(2,1)S(1)} %get-tuple-element.30.mine_ref), channel_id=1, source_target_pairs={{0,2},{1,3},{2,0},{3,1},{4,6},{5,7},{6,4},{7,5},{8,10},{9,11},{10,... | collective-permute-start | bytes 245768 | tf_op jit(solution)/shard_map/ppermute | solution.py:321
  94.9 4.4 %collective-permute-done.4.other_ref = bf16[4,80,128]{2,1,0:T(8,128)(2,1)S(1)} collective-permute-done((bf16[4,80,128]{2,1,0:T(8,128)(2,1)S(1)}, bf16[4,80,128]{2,1,0:T(8,128)(2,1)S(1)}, u32[]{:S(2)}, u32[]{:S(2)}) %collective-permute-start.4) | collective-permute-done | bytes 81952 | tf_op jit(solution)/shard_map/ppermute | solution.py:321
  99.3 2.9 %all-to-all-done.4.pieces_ref = bf16[16,48,128]{2,1,0:T(8,128)(2,1)S(1)} async-done(((bf16[16,48,128]{2,1,0:T(8,128)(2,1)}), bf16[16,48,128]{2,1,0:T(8,128)(2,1)S(1)}, u32[]{:S(2)}, u32[]{:S(2)}) %all-to-all-start.4) | async-done | bytes 196640 | tf_op jit(solution)/shard_map/all_to_all | solution.py:338
  102.3 0.8 shard_map.84
  (2 shorter events, 0.0 us)
Async XLA Ops:
  0.6 0.9 copy-start
  2.4 13.3 %all-to-all-start = ((bf16[8,288,128]{2,1,0:T(8,128)(2,1)}), bf16[8,288,128]{2,1,0:T(8,128)(2,1)S(1)}, u32[]{:S(2)}, u32[]{:S(2)}) async-start(bf16[8,288,128]{2,1,0:T(8,128)(2,1)} %broadcast_in_dim.2), calls=%async_computation | async-start | bytes 1179648 | tf_op jit(solution)/shard_map/all_to_all | solution.py:326
  8.3 1.3 %copy-start.1 = (bf16[128,4608]{1,0:T(8,128)(2,1)S(1)}, bf16[128,4608]{1,0:T(8,128)(2,1)}, u32[]{:S(2)}) copy-start(bf16[128,4608]{1,0:T(8,128)(2,1)} %q_ref.3) | copy-start | bytes 3538948
  9.6 1.2 %copy-start.3 = (bf16[128,4096]{1,0:T(8,128)(2,1)S(1)}, bf16[128,4096]{1,0:T(8,128)(2,1)}, u32[]{:S(2)}) copy-start(bf16[128,4096]{1,0:T(8,128)(2,1)} %g_ref.3) | copy-start | bytes 3145732
  10.8 0.7 copy-start.5
  11.5 13.5 %copy-start.6 = (bf16[576,128]{1,0:T(8,128)(2,1)S(1)}, bf16[576,128]{1,0:T(8,128)(2,1)}, u32[]{:S(2)}) copy-start(bf16[576,128]{1,0:T(8,128)(2,1)} %comp_ref.1) | copy-start | bytes 442372
  15.7 9.3 %copy-start.2 = (bf16[128,4608]{1,0:T(8,128)(2,1)S(1)}, bf16[128,4608]{1,0:T(8,128)(2,1)}, u32[]{:S(2)}) copy-start(bf16[128,4608]{1,0:T(8,128)(2,1)} %q_ref.3) | copy-start | bytes 3538948
  15.7 9.3 %copy-start.4 = (bf16[128,4096]{1,0:T(8,128)(2,1)S(1)}, bf16[128,4096]{1,0:T(8,128)(2,1)}, u32[]{:S(2)}) copy-start(bf16[128,4096]{1,0:T(8,128)(2,1)} %g_ref.3) | copy-start | bytes 3145732
  15.7 9.3 %collective-permute-start = (bf16[8,288,128]{2,1,0:T(8,128)(2,1)S(1)}, bf16[8,288,128]{2,1,0:T(8,128)(2,1)S(1)}, u32[]{:S(2)}, u32[]{:S(2)}) collective-permute-start(bf16[8,288,128]{2,1,0:T(8,128)(2,1)S(1)} %shard_map.77.mine_ref), channel_id=1, source_target_pairs={{0,8},{8,0},{1,9},{9,1},{2,10},{10,2},{3,11},{11,3},{4,12},{12,4},... | collective-permute-start | bytes 1769480 | tf_op jit(solution)/shard_map/ppermute | solution.py:321
  32.8 3.9 %collective-permute-start.1 = (bf16[8,288,128]{2,1,0:T(8,128)(2,1)S(1)}, bf16[8,288,128]{2,1,0:T(8,128)(2,1)S(1)}, u32[]{:S(2)}, u32[]{:S(2)}) collective-permute-start(bf16[8,288,128]{2,1,0:T(8,128)(2,1)S(1)} %get-tuple-element.23), channel_id=1, source_target_pairs={{0,8},{8,0},{1,9},{9,1},{2,10},{10,2},{3,11},{11,3},{4,12},{12,4},... | collective-permute-start | bytes 1769480 | tf_op jit(solution)/shard_map/ppermute | solution.py:321
  37.7 15.2 %all-to-all-start.1 = ((bf16[8,368,128]{2,1,0:T(8,128)(2,1)}), bf16[8,368,128]{2,1,0:T(8,128)(2,1)S(1)}, u32[]{:S(2)}, u32[]{:S(2)}) async-start(bf16[8,368,128]{2,1,0:T(8,128)(2,1)} %shard_map.80), calls=%async_computation.1 | async-start | bytes 1507328 | tf_op jit(solution)/shard_map/all_to_all | solution.py:331
  53.6 15.7 %all-to-all-start.2 = ((bf16[8,48,128]{2,1,0:T(8,128)(2,1)}), bf16[8,48,128]{2,1,0:T(8,128)(2,1)S(1)}, u32[]{:S(2)}, u32[]{:S(2)}) async-start(bf16[8,48,128]{2,1,0:T(8,128)(2,1)} %bitcast), calls=%async_computation.2 | async-start | bytes 196608 | tf_op jit(solution)/shard_map/all_to_all | solution.py:334
  61.6 4.7 %collective-permute-start.2 = (bf16[1,80,128]{2,1,0:T(8,128)(2,1)S(1)}, bf16[1,80,128]{2,1,0:T(8,128)(2,1)S(1)}, u32[]{:S(2)}, u32[]{:S(2)}) collective-permute-start(bf16[1,80,128]{2,1,0:T(8,128)(2,1)S(1)} %get-tuple-element.26.mine_ref), channel_id=1, source_target_pairs={{0,4},{4,0},{1,5},{5,1},{2,6},{6,2},{3,7},{7,3},{8,12},{12,8},{9,1... | collective-permute-start | bytes 61448 | tf_op jit(solution)/shard_map/ppermute | solution.py:321
  69.9 13.2 %all-to-all-start.3 = ((f32[4,48,128]{2,1,0:T(8,128)}), f32[4,48,128]{2,1,0:T(8,128)S(1)}, u32[]{:S(2)}, u32[]{:S(2)}) async-start(f32[4,48,128]{2,1,0:T(8,128)} %get-tuple-element.27), calls=%async_computation.3 | async-start | bytes 196608 | tf_op jit(solution)/shard_map/all_to_all | solution.py:336
  75.8 4.7 %collective-permute-start.3 = (bf16[2,80,128]{2,1,0:T(8,128)(2,1)S(1)}, bf16[2,80,128]{2,1,0:T(8,128)(2,1)S(1)}, u32[]{:S(2)}, u32[]{:S(2)}) collective-permute-start(bf16[2,80,128]{2,1,0:T(8,128)(2,1)S(1)} %get-tuple-element.28.mine_ref), channel_id=1, source_target_pairs={{0,1},{1,0},{2,3},{3,2},{4,5},{5,4},{6,7},{7,6},{8,9},{9,8},{10,11... | collective-permute-start | bytes 122888 | tf_op jit(solution)/shard_map/ppermute | solution.py:321
  83.8 18.4 %all-to-all-start.4 = ((bf16[16,48,128]{2,1,0:T(8,128)(2,1)}), bf16[16,48,128]{2,1,0:T(8,128)(2,1)S(1)}, u32[]{:S(2)}, u32[]{:S(2)}) async-start(bf16[16,48,128]{2,1,0:T(8,128)(2,1)} %get-tuple-element.29), calls=%async_computation.4 | async-start | bytes 393216 | tf_op jit(solution)/shard_map/all_to_all | solution.py:338
  91.9 7.4 %collective-permute-start.4 = (bf16[4,80,128]{2,1,0:T(8,128)(2,1)S(1)}, bf16[4,80,128]{2,1,0:T(8,128)(2,1)S(1)}, u32[]{:S(2)}, u32[]{:S(2)}) collective-permute-start(bf16[4,80,128]{2,1,0:T(8,128)(2,1)S(1)} %get-tuple-element.30.mine_ref), channel_id=1, source_target_pairs={{0,2},{1,3},{2,0},{3,1},{4,6},{5,7},{6,4},{7,5},{8,10},{9,11},{10,... | collective-permute-start | bytes 245768 | tf_op jit(solution)/shard_map/ppermute | solution.py:321

commit v5 on v4

--- a/solution.py
+++ b/solution.py
@@ -303,7 +303,7 @@
     for core in range(2):
         for j in range(HALF // SLICE):
             first = HALF * core + SLICE * j
-            prompt_ref[first : first + SLICE] = pieces_ref[2 * j + core].astype(F32)
+            prompt_ref[first : first + SLICE] = pieces_ref[8 * core + j].astype(F32)
 
 
 def finish(pieces, mine, other):
@@ -335,7 +335,7 @@
     pieces, comp = sum_and_join("yl", pieces, 4, F32, comp, swap(comp, "yl", 2, 1))
     pieces = lax.all_to_all(pieces, "yh", 0, 0)
     pieces, comp = sum_and_join("x", pieces, 16, BF, comp, swap(comp, "x", 4, 1))
-    pieces = lax.all_to_all(pieces, ("z", "c"), 0, 0)
+    pieces = lax.all_to_all(pieces, ("c", "z"), 0, 0)
     grad_prompt, grad_comp = finish(pieces, comp, swap(comp, "x", 4, 2))
     return (grad_queries, grad_prompt, grad_comp)
 

time: 104 us -> 102 us (0.981)
  waiting for transfers between devices: 29.7 us -> 27.7 us
    all_to_all x1, waiting for transfers between devices: 2.92 us -> 0.88 us  [on_device(): pieces = lax.all_to_all(pieces, ('c', 'z'), 0, 0)]
where the time goes in v5:
time: 102 us; the launch traced here: 101 us
  starting transfers between devices  49.6 us (49%)
  waiting for transfers between devices  27.7 us (27%)
  Pallas kernels  18.1 us (18%)
  local copies, waits for them, and re-layouts  4.96 us (5%)
    ppermute x5, starting transfers between devices, swap(): return lax.ppermute(block, axis, [(i, i ^ bit) for i in range(count)])  18.2 us
    ppermute x5, waiting for transfers between devices, swap(): return lax.ppermute(block, axis, [(i, i ^ bit) for i in range(count)])  11.7 us
    all_to_all x1, starting transfers between devices, on_device(): pieces = lax.all_to_all(pieces, ('c', 'z'), 0, 0)  8.1 us
    all_to_all x1, starting transfers between devices, on_device(): pieces = lax.all_to_all(prompt_part.reshape(8, SLICE, CLEN), 'z', 0, 0)  7.99 us
    pallas_call x1, Pallas kernels, main(): pl.pallas_call(main_kernel, out_shape=(jax.ShapeDtypeStruct((8, HALF, CLE...  7.76 us
    all_to_all x1, waiting for transfers between devices, on_device(): terms = lax.all_to_all(cores_sum(keep, swap(send, 'c', 2, 1)), HS, 0, 0)  6.56 us
    all_to_all x1, starting transfers between devices, on_device(): pieces = lax.all_to_all(pieces, 'yh', 0, 0)  5.91 us
    all_to_all x1, starting transfers between devices, on_device(): lax.all_to_all(jnp.broadcast_to(half[None], (8, HALF, CLEN)), HS, 0, 0)  5.86 us
  transfers between devices with their start and end apart: 10, of which 10 were waited for; matrix products, arithmetic and copies ran while one was open for 0% of the time, Pallas kernels for 6%

profile of v5, /device:TPU:1, one launch (start us, length us, event | category | flops | bytes accessed | tf_op | source)
XLA Modules:
  0.0 101.1 jit_solution(10370346249637251560)
XLA Ops:
  0.6 0.0 copy-start
  0.6 0.9 copy-done
  1.6 0.9 broadcast_in_dim.2
  2.4 5.9 %all-to-all-start = ((bf16[8,288,128]{2,1,0:T(8,128)(2,1)}), bf16[8,288,128]{2,1,0:T(8,128)(2,1)S(1)}, u32[]{:S(2)}, u32[]{:S(2)}) async-start(bf16[8,288,128]{2,1,0:T(8,128)(2,1)} %broadcast_in_dim.2), calls=%async_computation | async-start | bytes 1179648 | tf_op jit(solution)/shard_map/all_to_all | solution.py:326
  8.3 0.0 copy-start.1
  8.3 1.3 %copy-done.1 = bf16[128,4608]{1,0:T(8,128)(2,1)S(1)} copy-done((bf16[128,4608]{1,0:T(8,128)(2,1)S(1)}, bf16[128,4608]{1,0:T(8,128)(2,1)}, u32[]{:S(2)}) %copy-start.1) | copy-done | bytes 1179672
  9.6 0.0 copy-start.3
  9.6 1.2 %copy-done.3 = bf16[128,4096]{1,0:T(8,128)(2,1)S(1)} copy-done((bf16[128,4096]{1,0:T(8,128)(2,1)S(1)}, bf16[128,4096]{1,0:T(8,128)(2,1)}, u32[]{:S(2)}) %copy-start.3) | copy-done | bytes 1048600
  10.8 0.0 copy-start.5
  10.8 0.7 copy-done.5
  11.5 0.0 copy-start.6
  11.5 1.3 %shard_map.76 = (bf16[576,2048]{1,0:T(8,128)(2,1)S(1)}, f32[128,128]{1,0:T(8,128)S(1)}) custom-call(s32[64]{0:T(128)S(1)} %copy-done.5, bf16[128,4608]{1,0:T(8,128)(2,1)S(1)} %copy-done.1, bf16[128,4096]{1,0:T(8,128)(2,1)S(1)} %copy-done.3), custom_call_target="tpu_custom_call" | custom-call | bytes 4600000 | tf_op jit(solution)/shard_map/pallas_call | solution.py:57
  12.8 2.9 %all-to-all-done.block_ref = bf16[8,288,128]{2,1,0:T(8,128)(2,1)S(1)} async-done(((bf16[8,288,128]{2,1,0:T(8,128)(2,1)}), bf16[8,288,128]{2,1,0:T(8,128)(2,1)S(1)}, u32[]{:S(2)}, u32[]{:S(2)}) %all-to-all-start) | async-done | bytes 589856 | tf_op jit(solution)/shard_map/all_to_all | solution.py:326
  15.7 0.0 copy-start.2
  15.7 0.0 copy-start.4
  15.7 7.7 %collective-permute-start = (bf16[8,288,128]{2,1,0:T(8,128)(2,1)S(1)}, bf16[8,288,128]{2,1,0:T(8,128)(2,1)S(1)}, u32[]{:S(2)}, u32[]{:S(2)}) collective-permute-start(bf16[8,288,128]{2,1,0:T(8,128)(2,1)S(1)} %shard_map.77.mine_ref), channel_id=1, source_target_pairs={{0,8},{8,0},{1,9},{9,1},{2,10},{10,2},{3,11},{11,3},{4,12},{12,4},... | collective-permute-start | bytes 1769480 | tf_op jit(solution)/shard_map/ppermute | solution.py:321
  23.4 1.6 %collective-permute-done.other_ref = bf16[8,288,128]{2,1,0:T(8,128)(2,1)S(1)} collective-permute-done((bf16[8,288,128]{2,1,0:T(8,128)(2,1)S(1)}, bf16[8,288,128]{2,1,0:T(8,128)(2,1)S(1)}, u32[]{:S(2)}, u32[]{:S(2)}) %collective-permute-start) | collective-permute-done | bytes 589856 | tf_op jit(solution)/shard_map/ppermute | solution.py:321
  25.0 0.0 copy-done.6
  25.0 0.0 copy-done.2
  25.0 0.0 copy-done.4
  25.0 7.8 %shard_map.78 = (bf16[8,288,128]{2,1,0:T(8,128)(2,1)S(1)}, bf16[8,368,128]{2,1,0:T(8,128)(2,1)S(1)}, bf16[9216,1152]{1,0:T(8,128)(2,1)}) custom-call(f32[128,128]{1,0:T(8,128)S(1)} %get-tuple-element.18.alive_ref, bf16[128,4608]{1,0:T(8,128)(2,1)S(1)} %copy-done.2, bf16[128,4096]{1,0:T(8,128)(2,1)S(1)} %copy-done.4, ...), custom_call_target="tpu_custom_call" | custom-call | flops 5200000000 | bytes 12000000 | tf_op jit(solution)/shard_map/pallas_call | solution.py:154
  32.8 2.3 %collective-permute-start.1 = (bf16[8,288,128]{2,1,0:T(8,128)(2,1)S(1)}, bf16[8,288,128]{2,1,0:T(8,128)(2,1)S(1)}, u32[]{:S(2)}, u32[]{:S(2)}) collective-permute-start(bf16[8,288,128]{2,1,0:T(8,128)(2,1)S(1)} %get-tuple-element.23), channel_id=1, source_target_pairs={{0,8},{8,0},{1,9},{9,1},{2,10},{10,2},{3,11},{11,3},{4,12},{12,4},... | collective-permute-start | bytes 1769480 | tf_op jit(solution)/shard_map/ppermute | solution.py:321
  35.1 1.6 %collective-permute-done.1.got_ref = bf16[8,288,128]{2,1,0:T(8,128)(2,1)S(1)} collective-permute-done((bf16[8,288,128]{2,1,0:T(8,128)(2,1)S(1)}, bf16[8,288,128]{2,1,0:T(8,128)(2,1)S(1)}, u32[]{:S(2)}, u32[]{:S(2)}) %collective-permute-start.1) | collective-permute-done | bytes 589856 | tf_op jit(solution)/shard_map/ppermute | solution.py:321
  36.7 1.0 %shard_map.80 = bf16[8,368,128]{2,1,0:T(8,128)(2,1)} custom-call(bf16[8,368,128]{2,1,0:T(8,128)(2,1)S(1)} %get-tuple-element.22.keep_ref, bf16[8,288,128]{2,1,0:T(8,128)(2,1)S(1)} %collective-permute-done.1.got_ref), custom_call_target="tpu_custom_call" | custom-call | flops 300000 | bytes 2100000 | tf_op jit(solution)/shard_map/pallas_call | solution.py:228
  37.7 3.5 %all-to-all-start.1 = ((bf16[8,368,128]{2,1,0:T(8,128)(2,1)}), bf16[8,368,128]{2,1,0:T(8,128)(2,1)S(1)}, u32[]{:S(2)}, u32[]{:S(2)}) async-start(bf16[8,368,128]{2,1,0:T(8,128)(2,1)} %shard_map.80), calls=%async_computation.1 | async-start | bytes 1507328 | tf_op jit(solution)/shard_map/all_to_all | solution.py:331
  41.3 5.1 %shard_map.79 = (bf16[128,4608]{1,0:T(8,128)(2,1)}, bf16[9216,1152]{1,0:T(8,128)(2,1)}) custom-call(bf16[9216,1152]{1,0:T(8,128)(2,1)} %get-tuple-element.20.tall_hbm), custom_call_target="tpu_custom_call", output_to_operand_aliasing={{1}: (0, {})} | custom-call | flops 1400000000 | bytes 5000000 | tf_op jit(solution)/shard_map/pallas_call | solution.py:203
  46.3 6.6 %all-to-all-done.1.terms_ref = bf16[8,368,128]{2,1,0:T(8,128)(2,1)S(1)} async-done(((bf16[8,368,128]{2,1,0:T(8,128)(2,1)}), bf16[8,368,128]{2,1,0:T(8,128)(2,1)S(1)}, u32[]{:S(2)}, u32[]{:S(2)}) %all-to-all-start.1) | async-done | bytes 753696 | tf_op jit(solution)/shard_map/all_to_all | solution.py:331
  52.9 0.7 shard_map.81
  53.6 8.0 %all-to-all-start.2 = ((bf16[8,48,128]{2,1,0:T(8,128)(2,1)}), bf16[8,48,128]{2,1,0:T(8,128)(2,1)S(1)}, u32[]{:S(2)}, u32[]{:S(2)}) async-start(bf16[8,48,128]{2,1,0:T(8,128)(2,1)} %bitcast), calls=%async_computation.2 | async-start | bytes 196608 | tf_op jit(solution)/shard_map/all_to_all | solution.py:334
  61.6 3.2 %collective-permute-start.2 = (bf16[1,80,128]{2,1,0:T(8,128)(2,1)S(1)}, bf16[1,80,128]{2,1,0:T(8,128)(2,1)S(1)}, u32[]{:S(2)}, u32[]{:S(2)}) collective-permute-start(bf16[1,80,128]{2,1,0:T(8,128)(2,1)S(1)} %get-tuple-element.26.mine_ref), channel_id=1, source_target_pairs={{0,4},{4,0},{1,5},{5,1},{2,6},{6,2},{3,7},{7,3},{8,12},{12,8},{9,1... | collective-permute-start | bytes 61448 | tf_op jit(solution)/shard_map/ppermute | solution.py:321
  64.8 1.4 %collective-permute-done.2.other_ref = bf16[1,80,128]{2,1,0:T(8,128)(2,1)S(1)} collective-permute-done((bf16[1,80,128]{2,1,0:T(8,128)(2,1)S(1)}, bf16[1,80,128]{2,1,0:T(8,128)(2,1)S(1)}, u32[]{:S(2)}, u32[]{:S(2)}) %collective-permute-start.2) | collective-permute-done | bytes 20512 | tf_op jit(solution)/shard_map/ppermute | solution.py:321
  66.3 3.0 %all-to-all-done.2.pieces_ref = bf16[8,48,128]{2,1,0:T(8,128)(2,1)S(1)} async-done(((bf16[8,48,128]{2,1,0:T(8,128)(2,1)}), bf16[8,48,128]{2,1,0:T(8,128)(2,1)S(1)}, u32[]{:S(2)}, u32[]{:S(2)}) %all-to-all-start.2) | async-done | bytes 98336 | tf_op jit(solution)/shard_map/all_to_all | solution.py:334
  69.3 0.7 shard_map.82
  69.9 5.9 %all-to-all-start.3 = ((f32[4,48,128]{2,1,0:T(8,128)}), f32[4,48,128]{2,1,0:T(8,128)S(1)}, u32[]{:S(2)}, u32[]{:S(2)}) async-start(f32[4,48,128]{2,1,0:T(8,128)} %get-tuple-element.27), calls=%async_computation.3 | async-start | bytes 196608 | tf_op jit(solution)/shard_map/all_to_all | solution.py:336
  75.8 2.0 %collective-permute-start.3 = (bf16[2,80,128]{2,1,0:T(8,128)(2,1)S(1)}, bf16[2,80,128]{2,1,0:T(8,128)(2,1)S(1)}, u32[]{:S(2)}, u32[]{:S(2)}) collective-permute-start(bf16[2,80,128]{2,1,0:T(8,128)(2,1)S(1)} %get-tuple-element.28.mine_ref), channel_id=1, source_target_pairs={{0,1},{1,0},{2,3},{3,2},{4,5},{5,4},{6,7},{7,6},{8,9},{9,8},{10,11... | collective-permute-start | bytes 122888 | tf_op jit(solution)/shard_map/ppermute | solution.py:321
  77.9 2.7 %collective-permute-done.3.other_ref = bf16[2,80,128]{2,1,0:T(8,128)(2,1)S(1)} collective-permute-done((bf16[2,80,128]{2,1,0:T(8,128)(2,1)S(1)}, bf16[2,80,128]{2,1,0:T(8,128)(2,1)S(1)}, u32[]{:S(2)}, u32[]{:S(2)}) %collective-permute-start.3) | collective-permute-done | bytes 40992 | tf_op jit(solution)/shard_map/ppermute | solution.py:321
  80.6 2.6 %all-to-all-done.3.pieces_ref = f32[4,48,128]{2,1,0:T(8,128)S(1)} async-done(((f32[4,48,128]{2,1,0:T(8,128)}), f32[4,48,128]{2,1,0:T(8,128)S(1)}, u32[]{:S(2)}, u32[]{:S(2)}) %all-to-all-start.3) | async-done | bytes 98336 | tf_op jit(solution)/shard_map/all_to_all | solution.py:336
  83.1 0.7 shard_map.83
  83.8 8.1 %all-to-all-start.4 = ((bf16[16,48,128]{2,1,0:T(8,128)(2,1)}), bf16[16,48,128]{2,1,0:T(8,128)(2,1)S(1)}, u32[]{:S(2)}, u32[]{:S(2)}) async-start(bf16[16,48,128]{2,1,0:T(8,128)(2,1)} %get-tuple-element.29), calls=%async_computation.4 | async-start | bytes 393216 | tf_op jit(solution)/shard_map/all_to_all | solution.py:338
  91.9 3.0 %collective-permute-start.4 = (bf16[4,80,128]{2,1,0:T(8,128)(2,1)S(1)}, bf16[4,80,128]{2,1,0:T(8,128)(2,1)S(1)}, u32[]{:S(2)}, u32[]{:S(2)}) collective-permute-start(bf16[4,80,128]{2,1,0:T(8,128)(2,1)S(1)} %get-tuple-element.30.mine_ref), channel_id=1, source_target_pairs={{0,2},{1,3},{2,0},{3,1},{4,6},{5,7},{6,4},{7,5},{8,10},{9,11},{10,... | collective-permute-start | bytes 245768 | tf_op jit(solution)/shard_map/ppermute | solution.py:321
  94.9 4.4 %collective-permute-done.4.other_ref = bf16[4,80,128]{2,1,0:T(8,128)(2,1)S(1)} collective-permute-done((bf16[4,80,128]{2,1,0:T(8,128)(2,1)S(1)}, bf16[4,80,128]{2,1,0:T(8,128)(2,1)S(1)}, u32[]{:S(2)}, u32[]{:S(2)}) %collective-permute-start.4) | collective-permute-done | bytes 81952 | tf_op jit(solution)/shard_map/ppermute | solution.py:321
  99.3 0.9 all-to-all-done.4.pieces_ref
  100.2 0.8 shard_map.84
  (2 shorter events, 0.0 us)
Async XLA Ops:
  0.6 0.9 copy-start
  2.4 13.3 %all-to-all-start = ((bf16[8,288,128]{2,1,0:T(8,128)(2,1)}), bf16[8,288,128]{2,1,0:T(8,128)(2,1)S(1)}, u32[]{:S(2)}, u32[]{:S(2)}) async-start(bf16[8,288,128]{2,1,0:T(8,128)(2,1)} %broadcast_in_dim.2), calls=%async_computation | async-start | bytes 1179648 | tf_op jit(solution)/shard_map/all_to_all | solution.py:326
  8.3 1.3 %copy-start.1 = (bf16[128,4608]{1,0:T(8,128)(2,1)S(1)}, bf16[128,4608]{1,0:T(8,128)(2,1)}, u32[]{:S(2)}) copy-start(bf16[128,4608]{1,0:T(8,128)(2,1)} %q_ref.3) | copy-start | bytes 3538948
  9.6 1.2 %copy-start.3 = (bf16[128,4096]{1,0:T(8,128)(2,1)S(1)}, bf16[128,4096]{1,0:T(8,128)(2,1)}, u32[]{:S(2)}) copy-start(bf16[128,4096]{1,0:T(8,128)(2,1)} %g_ref.3) | copy-start | bytes 3145732
  10.8 0.7 copy-start.5
  11.5 13.5 %copy-start.6 = (bf16[576,128]{1,0:T(8,128)(2,1)S(1)}, bf16[576,128]{1,0:T(8,128)(2,1)}, u32[]{:S(2)}) copy-start(bf16[576,128]{1,0:T(8,128)(2,1)} %comp_ref.1) | copy-start | bytes 442372
  15.7 9.3 %copy-start.2 = (bf16[128,4608]{1,0:T(8,128)(2,1)S(1)}, bf16[128,4608]{1,0:T(8,128)(2,1)}, u32[]{:S(2)}) copy-start(bf16[128,4608]{1,0:T(8,128)(2,1)} %q_ref.3) | copy-start | bytes 3538948
  15.7 9.3 %copy-start.4 = (bf16[128,4096]{1,0:T(8,128)(2,1)S(1)}, bf16[128,4096]{1,0:T(8,128)(2,1)}, u32[]{:S(2)}) copy-start(bf16[128,4096]{1,0:T(8,128)(2,1)} %g_ref.3) | copy-start | bytes 3145732
  15.7 9.3 %collective-permute-start = (bf16[8,288,128]{2,1,0:T(8,128)(2,1)S(1)}, bf16[8,288,128]{2,1,0:T(8,128)(2,1)S(1)}, u32[]{:S(2)}, u32[]{:S(2)}) collective-permute-start(bf16[8,288,128]{2,1,0:T(8,128)(2,1)S(1)} %shard_map.77.mine_ref), channel_id=1, source_target_pairs={{0,8},{8,0},{1,9},{9,1},{2,10},{10,2},{3,11},{11,3},{4,12},{12,4},... | collective-permute-start | bytes 1769480 | tf_op jit(solution)/shard_map/ppermute | solution.py:321
  32.8 3.9 %collective-permute-start.1 = (bf16[8,288,128]{2,1,0:T(8,128)(2,1)S(1)}, bf16[8,288,128]{2,1,0:T(8,128)(2,1)S(1)}, u32[]{:S(2)}, u32[]{:S(2)}) collective-permute-start(bf16[8,288,128]{2,1,0:T(8,128)(2,1)S(1)} %get-tuple-element.23), channel_id=1, source_target_pairs={{0,8},{8,0},{1,9},{9,1},{2,10},{10,2},{3,11},{11,3},{4,12},{12,4},... | collective-permute-start | bytes 1769480 | tf_op jit(solution)/shard_map/ppermute | solution.py:321
  37.7 15.2 %all-to-all-start.1 = ((bf16[8,368,128]{2,1,0:T(8,128)(2,1)}), bf16[8,368,128]{2,1,0:T(8,128)(2,1)S(1)}, u32[]{:S(2)}, u32[]{:S(2)}) async-start(bf16[8,368,128]{2,1,0:T(8,128)(2,1)} %shard_map.80), calls=%async_computation.1 | async-start | bytes 1507328 | tf_op jit(solution)/shard_map/all_to_all | solution.py:331
  53.6 15.7 %all-to-all-start.2 = ((bf16[8,48,128]{2,1,0:T(8,128)(2,1)}), bf16[8,48,128]{2,1,0:T(8,128)(2,1)S(1)}, u32[]{:S(2)}, u32[]{:S(2)}) async-start(bf16[8,48,128]{2,1,0:T(8,128)(2,1)} %bitcast), calls=%async_computation.2 | async-start | bytes 196608 | tf_op jit(solution)/shard_map/all_to_all | solution.py:334
  61.6 4.7 %collective-permute-start.2 = (bf16[1,80,128]{2,1,0:T(8,128)(2,1)S(1)}, bf16[1,80,128]{2,1,0:T(8,128)(2,1)S(1)}, u32[]{:S(2)}, u32[]{:S(2)}) collective-permute-start(bf16[1,80,128]{2,1,0:T(8,128)(2,1)S(1)} %get-tuple-element.26.mine_ref), channel_id=1, source_target_pairs={{0,4},{4,0},{1,5},{5,1},{2,6},{6,2},{3,7},{7,3},{8,12},{12,8},{9,1... | collective-permute-start | bytes 61448 | tf_op jit(solution)/shard_map/ppermute | solution.py:321
  69.9 13.2 %all-to-all-start.3 = ((f32[4,48,128]{2,1,0:T(8,128)}), f32[4,48,128]{2,1,0:T(8,128)S(1)}, u32[]{:S(2)}, u32[]{:S(2)}) async-start(f32[4,48,128]{2,1,0:T(8,128)} %get-tuple-element.27), calls=%async_computation.3 | async-start | bytes 196608 | tf_op jit(solution)/shard_map/all_to_all | solution.py:336
  75.8 4.7 %collective-permute-start.3 = (bf16[2,80,128]{2,1,0:T(8,128)(2,1)S(1)}, bf16[2,80,128]{2,1,0:T(8,128)(2,1)S(1)}, u32[]{:S(2)}, u32[]{:S(2)}) collective-permute-start(bf16[2,80,128]{2,1,0:T(8,128)(2,1)S(1)} %get-tuple-element.28.mine_ref), channel_id=1, source_target_pairs={{0,1},{1,0},{2,3},{3,2},{4,5},{5,4},{6,7},{7,6},{8,9},{9,8},{10,11... | collective-permute-start | bytes 122888 | tf_op jit(solution)/shard_map/ppermute | solution.py:321
  83.8 16.4 %all-to-all-start.4 = ((bf16[16,48,128]{2,1,0:T(8,128)(2,1)}), bf16[16,48,128]{2,1,0:T(8,128)(2,1)S(1)}, u32[]{:S(2)}, u32[]{:S(2)}) async-start(bf16[16,48,128]{2,1,0:T(8,128)(2,1)} %get-tuple-element.29), calls=%async_computation.4 | async-start | bytes 393216 | tf_op jit(solution)/shard_map/all_to_all | solution.py:338
  91.9 7.4 %collective-permute-start.4 = (bf16[4,80,128]{2,1,0:T(8,128)(2,1)S(1)}, bf16[4,80,128]{2,1,0:T(8,128)(2,1)S(1)}, u32[]{:S(2)}, u32[]{:S(2)}) collective-permute-start(bf16[4,80,128]{2,1,0:T(8,128)(2,1)S(1)} %get-tuple-element.30.mine_ref), channel_id=1, source_target_pairs={{0,2},{1,3},{2,0},{3,1},{4,6},{5,7},{6,4},{7,5},{8,10},{9,11},{10,... | collective-permute-start | bytes 245768 | tf_op jit(solution)/shard_map/ppermute | solution.py:321
